TPU v7x, 32 devices: a whole 2x2x4 slice. The times are simulated.
32 devices in a mesh: dp: 16 (over z, x, core), tensor: 2 (over y).
Axes of the slice: x: 2, y: 2, z: 4, core: 2. Of those that a mesh axis runs over, the one named last changes fastest.
Arguments:
- tokens: bfloat16 [32768, 1024], P(('dp', 'tensor')), may hold values from -6 to 6
- cotangent: bfloat16 [32768, 1024], P(('dp', 'tensor')), may hold values from -6 to 6
- sequence_lengths: int32 [16, 2], P('dp'), may hold values from 0 to 2048, as said below
- sequence_starts: int32 [16, 2], P('dp'), may hold values from 0 to 2048, as said below
- weight_query: float32 [1024, 1024], P('dp', 'tensor'), may hold values from -0.1875 to 0.1875
- weight_key: float32 [1024, 1024], P('dp', 'tensor'), may hold values from -0.1875 to 0.1875
- weight_value: float32 [1024, 1024], P('dp', 'tensor'), may hold values from -0.1875 to 0.1875
- weight_dense: float32 [1024, 1024], P('dp', 'tensor'), may hold values from -2 to 2
- weight_in: float32 [1024, 4096], P('dp', 'tensor'), may hold values from -0.1875 to 0.1875
- weight_out: float32 [1024, 4096], P('dp', 'tensor'), may hold values from -0.09375 to 0.09375
- vectors: float32 [1024, 13], P('dp'), may hold values from -0.8 to 1.5, as said below
- first_query: float32 [1024, 1024], P('dp', 'tensor'), may hold values from -96 to 96
- first_key: float32 [1024, 1024], P('dp', 'tensor'), may hold values from -96 to 96
- first_value: float32 [1024, 1024], P('dp', 'tensor'), may hold values from -96 to 96
- first_dense: float32 [1024, 1024], P('dp', 'tensor'), may hold values from -8 to 8
- first_in: float32 [1024, 4096], P('dp', 'tensor'), may hold values from -32 to 32
- first_out: float32 [1024, 4096], P('dp', 'tensor'), may hold values from -80 to 80
- first_vectors: float32 [1024, 13], P('dp'), may hold values from -114.04218 to 114.04218
- second_query: float32 [1024, 1024], P('dp', 'tensor'), may hold values from 1114.112 to 4423.68
- second_key: float32 [1024, 1024], P('dp', 'tensor'), may hold values from 1114.112 to 4423.68
- second_value: float32 [1024, 1024], P('dp', 'tensor'), may hold values from 1114.112 to 4423.68
- second_dense: float32 [1024, 1024], P('dp', 'tensor'), may hold values from 8.416 to 33.6
- second_in: float32 [1024, 4096], P('dp', 'tensor'), may hold values from 154.0096 to 622.592
- second_out: float32 [1024, 4096], P('dp', 'tensor'), may hold values from 720.896 to 2916.352
- second_vectors: float32 [1024, 13], P('dp'), may hold values from 154.0096 to 13762.56
Outputs:
- output: bfloat16 [32768, 1024], P(('dp', 'tensor'))
- input_grad: bfloat16 [32768, 1024], P(('dp', 'tensor'))
- next_first_query: float32 [1024, 1024], P('dp', 'tensor')
- next_first_key: float32 [1024, 1024], P('dp', 'tensor')
- next_first_value: float32 [1024, 1024], P('dp', 'tensor')
- next_first_dense: float32 [1024, 1024], P('dp', 'tensor')
- next_first_in: float32 [1024, 4096], P('dp', 'tensor')
- next_first_out: float32 [1024, 4096], P('dp', 'tensor')
- next_first_vectors: float32 [1024, 13], P('dp')
- next_second_query: float32 [1024, 1024], P('dp', 'tensor')
- next_second_key: float32 [1024, 1024], P('dp', 'tensor')
- next_second_value: float32 [1024, 1024], P('dp', 'tensor')
- next_second_dense: float32 [1024, 1024], P('dp', 'tensor')
- next_second_in: float32 [1024, 4096], P('dp', 'tensor')
- next_second_out: float32 [1024, 4096], P('dp', 'tensor')
- next_second_vectors: float32 [1024, 13], P('dp')
- next_weight_query: float32 [1024, 1024], P('dp', 'tensor')
- next_weight_key: float32 [1024, 1024], P('dp', 'tensor')
- next_weight_value: float32 [1024, 1024], P('dp', 'tensor')
- next_weight_dense: float32 [1024, 1024], P('dp', 'tensor')
- next_weight_in: float32 [1024, 4096], P('dp', 'tensor')
- next_weight_out: float32 [1024, 4096], P('dp', 'tensor')
- next_vectors: float32 [1024, 13], P('dp')
Inputs may be any that keep to these rules, and one draw needn't show every extreme that they name: `sequence_lengths`: in each group the sequences occupy disjoint slots within its 2048 rows, the second after the first; the first covers rows 1023 and 1024; a length 0 marks an unused slot; some group holds a single sequence of 2048. `sequence_starts`: the offsets that go with sequence_lengths. `vectors`: gains in columns 0 and 2, biases elsewhere.
All inputs are finite; a program needn't handle non-finite values.
Results may differ from a plain program's by a relative error of at most 0.012.
The roundings to bfloat16 on the way count: a program that leaves them out, or rounds other values in their place, can miss the bound.
Values may be sent and summed in bfloat16 or wider, within the bound.
A program may use at most 320 MiB of HBM per device.

v0:
```python
import jax
import jax.numpy as jnp
from jax import lax
from jax.sharding import PartitionSpec as P

HEAD_DIM = 64
ROT = 16
STEP = 10


NORM_EPS = 1e-05
BETA_FIRST = 0.9
BETA_SECOND = 0.95
ADAM_EPS = 1e-08
WEIGHT_DECAY = 0.01
RATE_MATRIX = 0.04
RATE_DENSE = 0.2
RATE_VECTOR = 0.5
MASKED = -1000000000.0


def layout(lengths, offsets, total_rows):
    row_ids = jnp.arange(total_rows, dtype=jnp.int32)
    inside = (
        (row_ids[:, None] >= offsets[None, :])
        & (row_ids[:, None] < offsets[None, :] + lengths[None, :])
    ).astype(jnp.int32)
    slot_ids = jnp.arange(lengths.shape[0], dtype=jnp.int32)
    member = jnp.sum(inside, axis=1)
    segment = jnp.where(
        member > 0, jnp.sum(inside * slot_ids[None, :], axis=1), lengths.shape[0] + row_ids
    )
    position = jnp.where(member > 0, row_ids - jnp.sum(inside * offsets[None, :], axis=1), 0)
    return (segment, position)


def rotate(heads, position):
    half = ROT // 2
    freq = 10000.0 ** (-2.0 * jnp.arange(half, dtype=jnp.float32) / ROT)
    angle = position.astype(jnp.float32)[:, None] * freq[None, :]
    cosine = jnp.cos(angle)[:, None, :]
    sine = jnp.sin(angle)[:, None, :]
    lower = heads[..., :half]
    upper = heads[..., half:ROT]
    return jnp.concatenate(
        [lower * cosine - upper * sine, upper * cosine + lower * sine, heads[..., ROT:]], axis=-1
    )


def layer_norm(values, gain, shift):
    centred = values - jnp.mean(values, axis=-1, keepdims=True)
    spread = jnp.mean(centred * centred, axis=-1, keepdims=True)
    return centred * lax.rsqrt(spread + NORM_EPS) * gain + shift


def normalize_pair(values, gain_one, shift_one, gain_two, shift_two):
    return (layer_norm(values, gain_one, shift_one), layer_norm(values, gain_two, shift_two))


def exact_gelu(values):
    return jax.nn.gelu(values, approximate=False)


def adam_update(weight_matrix, grad, first, second, rate, decay):
    first = BETA_FIRST * first + (1.0 - BETA_FIRST) * grad
    second = BETA_SECOND * second + (1.0 - BETA_SECOND) * grad * grad
    fixed_first = first / (1.0 - BETA_FIRST**STEP)
    fixed_second = second / (1.0 - BETA_SECOND**STEP)
    weight_matrix = weight_matrix - rate * (
        fixed_first / (jnp.sqrt(fixed_second) + ADAM_EPS) + decay * weight_matrix
    )
    return (first, second, weight_matrix)


def shards(
    tokens,
    cotangent,
    sequence_lengths,
    sequence_starts,
    weight_query,
    weight_key,
    weight_value,
    weight_dense,
    weight_in,
    weight_out,
    vectors,
    first_query,
    first_key,
    first_value,
    first_dense,
    first_in,
    first_out,
    first_vectors,
    second_query,
    second_key,
    second_value,
    second_dense,
    second_in,
    second_out,
    second_vectors,
):
    tensor_size = lax.axis_size("tensor")
    tensor_rank = lax.axis_index("tensor")
    shard_rows, model_width = tokens.shape
    all_rows = shard_rows * tensor_size
    segment, position = layout(sequence_lengths[0], sequence_starts[0], all_rows)
    masters = (weight_query, weight_key, weight_value, weight_dense, weight_in, weight_out, vectors)
    copies = [master.astype(jnp.bfloat16) for master in masters]
    gathered = (
        lax.all_gather(copies[0], "dp", axis=0, tiled=True),
        lax.all_gather(copies[1], "dp", axis=0, tiled=True),
        lax.all_gather(copies[2], "dp", axis=0, tiled=True),
        lax.all_gather(copies[3], "dp", axis=0, tiled=True),
        lax.all_gather(copies[4], "dp", axis=0, tiled=True),
        lax.all_gather(copies[5], "dp", axis=0, tiled=True),
        lax.all_gather(copies[6], "dp", axis=0, tiled=True),
    )
    query_full, key_full, value_full, dense_full, in_full, out_full = gathered[:6]
    vector_copy = gathered[6].astype(jnp.float32)
    columns = [vector_copy[:, column] for column in range(9)]
    (
        gain_one,
        shift_one,
        gain_two,
        shift_two,
        bias_dense,
        bias_out,
        query_bias_all,
        key_bias_all,
        value_bias_all,
    ) = columns
    head_cols = query_full.shape[1]
    hidden_cols = in_full.shape[1]
    heads_here = head_cols // HEAD_DIM
    bias_query = lax.dynamic_slice_in_dim(query_bias_all, tensor_rank * head_cols, head_cols)
    bias_key = lax.dynamic_slice_in_dim(key_bias_all, tensor_rank * head_cols, head_cols)
    bias_value = lax.dynamic_slice_in_dim(value_bias_all, tensor_rank * head_cols, head_cols)
    bias_in = lax.dynamic_slice_in_dim(
        vector_copy[:, 9:].T.reshape(-1), tensor_rank * hidden_cols, hidden_cols
    )
    whole_rows = lax.all_gather(tokens, "tensor", axis=0, tiled=True)
    rows_float = whole_rows.astype(jnp.float32)
    normed_one_f, normed_two_f = normalize_pair(
        rows_float, gain_one, shift_one, gain_two, shift_two
    )
    normed_one = normed_one_f.astype(jnp.bfloat16)
    normed_two = normed_two_f.astype(jnp.bfloat16)

    def project(weight_matrix, bias):
        return (
            jnp.dot(normed_one, weight_matrix, preferred_element_type=jnp.float32) + bias
        ).reshape(all_rows, heads_here, HEAD_DIM)

    query_lin = project(query_full, bias_query)
    key_lin = project(key_full, bias_key)
    query_rows = rotate(query_lin, position).astype(jnp.bfloat16)
    key_rows = rotate(key_lin, position).astype(jnp.bfloat16)
    value_rows = project(value_full, bias_value).astype(jnp.bfloat16)
    block_rows = min(512, all_rows)
    block_count = all_rows // block_rows
    score_scale = HEAD_DIM ** (-0.5)
    col_ids = jnp.arange(all_rows, dtype=jnp.int32)
    starts = jnp.arange(block_count, dtype=jnp.int32) * block_rows

    def masked_scores(query_block, start):
        block_ids = start + jnp.arange(block_rows, dtype=jnp.int32)
        block_segment = lax.dynamic_slice_in_dim(segment, start, block_rows, 0)
        allowed = (block_segment[:, None] == segment[None, :]) & (
            col_ids[None, :] <= block_ids[:, None]
        )
        scores = (
            jnp.einsum("qhd,khd->hqk", query_block, key_rows, preferred_element_type=jnp.float32)
            * score_scale
        )
        return jnp.where(allowed[None], scores, MASKED)

    def forward_block(start):
        query_block = lax.dynamic_slice_in_dim(query_rows, start, block_rows, 0)
        scores = masked_scores(query_block, start)
        row_max = jnp.max(scores, axis=-1, keepdims=True)
        exps = jnp.exp(scores - row_max)
        row_total = jnp.sum(exps, axis=-1, keepdims=True)
        probs_low = (exps / row_total).astype(jnp.bfloat16)
        block_out = jnp.einsum(
            "hqk,khd->qhd", probs_low, value_rows, preferred_element_type=jnp.float32
        )
        return (block_out.astype(jnp.bfloat16), (row_max + jnp.log(row_total))[..., 0])

    attended_blocks, log_totals = lax.map(forward_block, starts)
    attended = attended_blocks.reshape(all_rows, head_cols)
    hidden_pre = jnp.dot(normed_two, in_full, preferred_element_type=jnp.float32) + bias_in
    activated = exact_gelu(hidden_pre).astype(jnp.bfloat16)
    mixed = jnp.einsum("gf,df->gd", attended, dense_full, preferred_element_type=jnp.float32)
    mixed = mixed + jnp.einsum("gf,df->gd", activated, out_full, preferred_element_type=jnp.float32)
    branches = lax.psum_scatter(mixed, "tensor", scatter_dimension=0, tiled=True)
    output = (tokens.astype(jnp.float32) + branches + bias_dense + bias_out).astype(jnp.bfloat16)
    regathered = (
        lax.all_gather(copies[0], "dp", axis=0, tiled=True),
        lax.all_gather(copies[1], "dp", axis=0, tiled=True),
        lax.all_gather(copies[2], "dp", axis=0, tiled=True),
        lax.all_gather(copies[3], "dp", axis=0, tiled=True),
        lax.all_gather(copies[4], "dp", axis=0, tiled=True),
        lax.all_gather(copies[5], "dp", axis=0, tiled=True),
    )
    query_full, key_full, value_full, dense_full, in_full, out_full = regathered
    grad_rows = lax.all_gather(cotangent, "tensor", axis=0, tiled=True)
    grad_dense = jnp.einsum("gd,gf->df", grad_rows, attended, preferred_element_type=jnp.float32)
    grad_out = jnp.einsum("gd,gf->df", grad_rows, activated, preferred_element_type=jnp.float32)
    grad_activated = jnp.dot(grad_rows, out_full, preferred_element_type=jnp.float32)
    gelu_pull = jax.vjp(exact_gelu, hidden_pre)[1]
    grad_pre = gelu_pull(grad_activated)[0].astype(jnp.bfloat16)
    grad_in = jnp.einsum("gd,gf->df", normed_two, grad_pre, preferred_element_type=jnp.float32)
    grad_two = jnp.einsum("gf,df->gd", grad_pre, in_full, preferred_element_type=jnp.float32)
    grad_attended = jnp.dot(grad_rows, dense_full, preferred_element_type=jnp.float32).astype(
        jnp.bfloat16
    )
    grad_attended = grad_attended.reshape(all_rows, heads_here, HEAD_DIM)

    def backward_block(carry, block_item):
        grad_key_sum, grad_value_sum = carry
        start, log_block = block_item
        query_block = lax.dynamic_slice_in_dim(query_rows, start, block_rows, 0)
        grad_block = lax.dynamic_slice_in_dim(grad_attended, start, block_rows, 0)
        probs = jnp.exp(masked_scores(query_block, start) - log_block[..., None])
        grad_probs = jnp.einsum(
            "qhd,khd->hqk", grad_block, value_rows, preferred_element_type=jnp.float32
        )
        centre = jnp.sum(probs * grad_probs, axis=-1, keepdims=True)
        grad_scores = (probs * (grad_probs - centre)).astype(jnp.bfloat16)
        grad_query_block = (
            jnp.einsum("hqk,khd->qhd", grad_scores, key_rows, preferred_element_type=jnp.float32)
            * score_scale
        )
        grad_key_sum = (
            grad_key_sum
            + jnp.einsum(
                "hqk,qhd->khd", grad_scores, query_block, preferred_element_type=jnp.float32
            )
            * score_scale
        )
        grad_value_sum = grad_value_sum + jnp.einsum(
            "hqk,qhd->khd",
            probs.astype(jnp.bfloat16),
            grad_block,
            preferred_element_type=jnp.float32,
        )
        return ((grad_key_sum, grad_value_sum), grad_query_block)

    zero_heads = jnp.zeros((all_rows, heads_here, HEAD_DIM), jnp.float32)
    (grad_key, grad_value), grad_query_blocks = lax.scan(
        backward_block, (zero_heads, zero_heads), (starts, log_totals)
    )
    grad_query = grad_query_blocks.reshape(all_rows, heads_here, HEAD_DIM)
    rotary_pull = jax.vjp(lambda inner: rotate(inner, position), query_lin)[1]
    grad_query_lin = rotary_pull(grad_query)[0].astype(jnp.bfloat16).reshape(all_rows, head_cols)
    grad_key_lin = rotary_pull(grad_key)[0].astype(jnp.bfloat16).reshape(all_rows, head_cols)
    grad_value_lin = grad_value.astype(jnp.bfloat16).reshape(all_rows, head_cols)
    grad_query_weight = jnp.einsum(
        "gd,gf->df", normed_one, grad_query_lin, preferred_element_type=jnp.float32
    )
    grad_key_weight = jnp.einsum(
        "gd,gf->df", normed_one, grad_key_lin, preferred_element_type=jnp.float32
    )
    grad_value_weight = jnp.einsum(
        "gd,gf->df", normed_one, grad_value_lin, preferred_element_type=jnp.float32
    )
    grad_one = jnp.einsum(
        "gf,df->gd", grad_query_lin, query_full, preferred_element_type=jnp.float32
    )
    grad_one = grad_one + jnp.einsum(
        "gf,df->gd", grad_key_lin, key_full, preferred_element_type=jnp.float32
    )
    grad_one = grad_one + jnp.einsum(
        "gf,df->gd", grad_value_lin, value_full, preferred_element_type=jnp.float32
    )
    norm_pull = jax.vjp(normalize_pair, rows_float, gain_one, shift_one, gain_two, shift_two)[1]
    grad_rows_part, grad_gain_one, grad_shift_one, grad_gain_two, grad_shift_two = norm_pull(
        (grad_one, grad_two)
    )
    grad_from_norms = lax.psum_scatter(grad_rows_part, "tensor", scatter_dimension=0, tiled=True)
    input_grad = (cotangent.astype(jnp.float32) + grad_from_norms).astype(jnp.bfloat16)

    def placed(values, total_len):
        return lax.dynamic_update_slice(
            jnp.zeros((total_len,), jnp.float32), values, (tensor_rank * values.shape[0],)
        )

    local_bias = jnp.sum(cotangent.astype(jnp.float32), axis=0)
    grad_bias_query = placed(jnp.sum(grad_query_lin.astype(jnp.float32), axis=0), model_width)
    grad_bias_key = placed(jnp.sum(grad_key_lin.astype(jnp.float32), axis=0), model_width)
    grad_bias_value = placed(jnp.sum(grad_value_lin.astype(jnp.float32), axis=0), model_width)
    grad_bias_in = placed(jnp.sum(grad_pre.astype(jnp.float32), axis=0), hidden_cols * tensor_size)
    grad_vector = jnp.concatenate(
        [
            jnp.stack(
                [
                    grad_gain_one,
                    grad_shift_one,
                    grad_gain_two,
                    grad_shift_two,
                    local_bias,
                    local_bias,
                    grad_bias_query,
                    grad_bias_key,
                    grad_bias_value,
                ],
                axis=1,
            ),
            grad_bias_in.reshape(-1, model_width).T,
        ],
        axis=1,
    )
    reduced = (
        lax.psum_scatter(grad_query_weight, "dp", scatter_dimension=0, tiled=True),
        lax.psum_scatter(grad_key_weight, "dp", scatter_dimension=0, tiled=True),
        lax.psum_scatter(grad_value_weight, "dp", scatter_dimension=0, tiled=True),
        lax.psum_scatter(grad_dense, "dp", scatter_dimension=0, tiled=True),
        lax.psum_scatter(grad_in, "dp", scatter_dimension=0, tiled=True),
        lax.psum_scatter(grad_out, "dp", scatter_dimension=0, tiled=True),
        lax.psum_scatter(grad_vector, "dp", scatter_dimension=0, tiled=True),
    )
    vector_grad = lax.psum(reduced[6], "tensor")
    grads = (reduced[0], reduced[1], reduced[2], reduced[3], reduced[4], reduced[5], vector_grad)
    firsts = (first_query, first_key, first_value, first_dense, first_in, first_out, first_vectors)
    seconds = (
        second_query,
        second_key,
        second_value,
        second_dense,
        second_in,
        second_out,
        second_vectors,
    )
    rates = (
        RATE_MATRIX,
        RATE_MATRIX,
        RATE_MATRIX,
        RATE_DENSE,
        RATE_MATRIX,
        RATE_MATRIX,
        RATE_VECTOR,
    )
    decays = (
        WEIGHT_DECAY,
        WEIGHT_DECAY,
        WEIGHT_DECAY,
        WEIGHT_DECAY,
        WEIGHT_DECAY,
        WEIGHT_DECAY,
        0.0,
    )
    updated = [
        adam_update(
            masters[slot], grads[slot], firsts[slot], seconds[slot], rates[slot], decays[slot]
        )
        for slot in range(7)
    ]
    return (
        output,
        input_grad,
        updated[0][0],
        updated[1][0],
        updated[2][0],
        updated[3][0],
        updated[4][0],
        updated[5][0],
        updated[6][0],
        updated[0][1],
        updated[1][1],
        updated[2][1],
        updated[3][1],
        updated[4][1],
        updated[5][1],
        updated[6][1],
        updated[0][2],
        updated[1][2],
        updated[2][2],
        updated[3][2],
        updated[4][2],
        updated[5][2],
        updated[6][2],
    )


def solution(mesh):
    in_specs = (
        P(("dp", "tensor"), None),
        P(("dp", "tensor"), None),
        P("dp", None),
        P("dp", None),
        P("dp", "tensor"),
        P("dp", "tensor"),
        P("dp", "tensor"),
        P("dp", "tensor"),
        P("dp", "tensor"),
        P("dp", "tensor"),
        P("dp", None),
        P("dp", "tensor"),
        P("dp", "tensor"),
        P("dp", "tensor"),
        P("dp", "tensor"),
        P("dp", "tensor"),
        P("dp", "tensor"),
        P("dp", None),
        P("dp", "tensor"),
        P("dp", "tensor"),
        P("dp", "tensor"),
        P("dp", "tensor"),
        P("dp", "tensor"),
        P("dp", "tensor"),
        P("dp", None),
    )
    out_specs = (
        P(("dp", "tensor"), None),
        P(("dp", "tensor"), None),
        P("dp", "tensor"),
        P("dp", "tensor"),
        P("dp", "tensor"),
        P("dp", "tensor"),
        P("dp", "tensor"),
        P("dp", "tensor"),
        P("dp", None),
        P("dp", "tensor"),
        P("dp", "tensor"),
        P("dp", "tensor"),
        P("dp", "tensor"),
        P("dp", "tensor"),
        P("dp", "tensor"),
        P("dp", None),
        P("dp", "tensor"),
        P("dp", "tensor"),
        P("dp", "tensor"),
        P("dp", "tensor"),
        P("dp", "tensor"),
        P("dp", "tensor"),
        P("dp", None),
    )
    return jax.shard_map(shards, mesh=mesh, in_specs=in_specs, out_specs=out_specs, check_vma=False)
```

profile of v0, /device:TPU:0, one launch (start us, length us, event | category | flops | bytes accessed | tf_op | source)
XLA Modules:
  0.0 1841.1 jit_solution(9620004962798762194)
XLA Ops:
  14.2 23.2 %all-gather = bf16[16,64,13]{1,2,0:T(8,128)(2,1)S(1)} all-gather(bf16[1,64,13]{1,2,0:T(8,128)(2,1)S(1)} %convert_bitcast_fusion), channel_id=1, replica_groups=mesh['dp'=16,'tensor'=2] {'dp'}, dimensions={0}, use_global_device_ids=true | all-gather | bytes 28288 | tf_op jit(solution)/shard_map/all_gather | solution.py:116
  40.0 29.0 %all-gather.10.cloned.1.call-done = bf16[2048,1024]{1,0:T(8,128)(2,1)} async-done(((bf16[1024,1024]{1,0:T(8,128)(2,1)}), bf16[2048,1024]{1,0:T(8,128)(2,1)}) %all-gather.10.cloned.1.call-update) | async-done | bytes 4194320 | tf_op jit(solution)/shard_map/all_gather | solution.py:141
  78.2 31.6 %all-gather.14.cloned.1.call-done = bf16[1024,512]{1,0:T(8,128)(2,1)} async-done(((bf16[64,512]{1,0:T(8,128)(2,1)}), bf16[1024,512]{1,0:T(8,128)(2,1)}) %all-gather.14.cloned.1.call-update) | async-done | bytes 1048592 | tf_op jit(solution)/shard_map/all_gather | solution.py:111
  118.2 31.2 %all-gather.12.cloned.1.call-done = bf16[1024,512]{1,0:T(8,128)(2,1)} async-done(((bf16[64,512]{1,0:T(8,128)(2,1)}), bf16[1024,512]{1,0:T(8,128)(2,1)}) %all-gather.12.cloned.1.call-update) | async-done | bytes 1048592 | tf_op jit(solution)/shard_map/all_gather | solution.py:110
  157.8 31.1 %all-gather.16.cloned.1.call-done = bf16[1024,512]{1,0:T(8,128)(2,1)} async-done(((bf16[64,512]{1,0:T(8,128)(2,1)}), bf16[1024,512]{1,0:T(8,128)(2,1)}) %all-gather.16.cloned.1.call-update) | async-done | bytes 1048592 | tf_op jit(solution)/shard_map/all_gather | solution.py:112
  195.1 204.6 %while.28 = (s32[]{:T(128)}, bf16[4,512,8,64]{1,3,2,0:T(8,128)(2,1)}, f32[4,8,512]{2,1,0:T(8,128)}, s32[4]{0:T(128)S(1)}, s32[2048]{0:T(1024)S(1)}, /*index=5*/b...) while((s32[]{:T(128)}, ...), condition=%wide.region_8.9_spmd.clone, body=%wide.region_5.0_spmd.clone.sunk | while | flops 2251551232 | bytes 110251176 | solution.py:189
  199.8 15.5 fusion.151
  215.3 15.0 fusion.152
  230.9 15.5 fusion.153
  250.9 15.5 fusion.151
  266.4 15.0 fusion.152
  282.0 15.5 fusion.153
  302.0 15.5 fusion.151
  317.5 15.0 fusion.152
  333.1 15.5 fusion.153
  353.1 15.4 fusion.151
  368.5 15.0 fusion.152
  384.1 15.5 fusion.153
  414.0 59.0 %reduce-scatter.22.cloned.1.call-done = f32[64,512]{1,0:T(8,128)} async-done(((f32[1024,512]{1,0:T(8,128)}), f32[64,512]{1,0:T(8,128)}) %reduce-scatter.22.cloned.1.call-update) | async-done | bytes 131088 | tf_op jit(solution)/shard_map/reduce_scatter | solution.py:317
  474.8 50.8 %all-gather.20.cloned.1.call-done = bf16[1024,2048]{1,0:T(8,128)(2,1)} async-done(((bf16[64,2048]{1,0:T(8,128)(2,1)}), bf16[1024,2048]{1,0:T(8,128)(2,1)}) %all-gather.20.cloned.1.call-update) | async-done | bytes 4194320 | tf_op jit(solution)/shard_map/all_gather | solution.py:114
  525.6 59.9 %multiply_convert_fusion.1 = (bf16[2048,2048]{1,0:T(8,128)(2,1)S(1)}, f32[2048,2048]{1,0:T(8,128)}, f32[2048,2048]{1,0:T(8,128)}) fusion(f32[2048]{0:T(1024)S(1)} %dynamic_slice.41, bf16[1024,2048]{1,0:T(8,128)(2,1)} %all-gather.20.cloned.1.call-done, bf16[2048,1024]{1,0:T(8,128)(2,1)} %all-gather.10.cloned.1.call-done, f32[1024]{0:T(1024)S(1)} %bitcast.173, ...), kind=kOutput, calls=%fused_computation.46 | convolution fusion | flops 8879341568 | bytes 50364416 | tf_op jit(solution)/shard_map/dot_general | solution.py:191
  588.8 11.3 convolution_bitcast_fusion
  606.7 96.8 %reduce-scatter.26.cloned.1.call-done = f32[64,2048]{1,0:T(8,128)} async-done(((f32[1024,2048]{1,0:T(8,128)}), f32[64,2048]{1,0:T(8,128)}) %reduce-scatter.26.cloned.1.call-update) | async-done | bytes 524304 | tf_op jit(solution)/shard_map/reduce_scatter | solution.py:319
  706.3 544.5 %while.29 = (s32[]{:T(128)}, f32[2048,8,64]{0,2,1:T(8,128)}, f32[2048,8,64]{0,2,1:T(8,128)}, f32[4,512,8,64]{1,0,3,2:T(4,128)}, s32[4]{0:T(128)S(1)}, /*index=5*...) while((s32[]{:T(128)}, f32[2048,8,64]{0,2,1:T(8,128)}, ...), condition=%wide.region_14.15_spmd.clone, body=%wide.region_12.14_spmd.clone.sunk | while | flops 5452853760 | bytes 284264640 | solution.py:250
  711.1 17.6 fusion.163
  729.5 26.4 %multiply_reduce_fusion.2 = (f32[8,512]{1,0:T(8,128)S(1)}, f32[8,512,2048]{2,1,0:T(8,128)}) fusion(f32[8,512,2048]{2,1,0:T(8,128)} %fusion.163, f32[8,512]{1,0:T(8,128)S(1)} %dynamic-slice_bitcast_fusion.2, bf16[2048,8,64]{0,2,1:T(8,128)(2,1)S(1)} %get-tuple-element.511, bf16[2048,8,64]{0,2,1:T(8,128)(2,1)} %get-tuple-element.509, ...), kind=kOutput, calls=%fused_computation.21.clone.1 | convolution fusion | flops 1115680768 | bytes 70811648 | tf_op jit(solution)/shard_map/while/body/eval_jaxpr/qhd,khd->hqk/dot_general | solution.py:172
  755.9 27.4 %multiply_convert_fusion.3 = bf16[8,512,2048]{2,1,0:T(8,128)(2,1)} fusion(f32[8,512,2048]{2,1,0:T(8,128)} %get-tuple-element.441, f32[8,512,2048]{2,1,0:T(8,128)} %fusion.163, f32[8,512]{1,0:T(8,128)S(1)} %get-tuple-element.442), kind=kLoop, calls=%fused_computation.20.clone.1 | loop fusion | flops 25165824 | bytes 83902464 | tf_op jit(solution)/shard_map/while/body/eval_jaxpr/convert_element_type | solution.py:229
  783.2 8.7 fusion.165
  793.1 21.0 %dynamic_update_slice.44 = f32[4,512,8,64]{1,0,3,2:T(4,128)} dynamic-update-slice(f32[4,512,8,64]{1,0,3,2:T(4,128)} %get-tuple-element.493, f32[1,512,8,64]{1,0,3,2:T(1,128)S(1)} %copy.103, s32[]{:T(128)} %get-tuple-element.490, s32[]{:T(128)} %constant.84.clone.1..sunk.1, s32[]{:T(128)} %constant.84.clone.1..sunk.1, s32[]{:T(128)} %constant.84.clone.1..sunk.1) | dynamic-update-slice | bytes 2097156 | tf_op jit(solution)/shard_map/while/body/jit(dynamic_update_index_in_dim)/dynamic_update_slice | solution.py:250
  814.1 11.0 bitcast_add_fusion.4
  825.1 15.9 bitcast_add_fusion.5
  845.5 17.5 fusion.163
  863.7 26.4 %multiply_reduce_fusion.2 = (f32[8,512]{1,0:T(8,128)S(1)}, f32[8,512,2048]{2,1,0:T(8,128)}) fusion(f32[8,512,2048]{2,1,0:T(8,128)} %fusion.163, f32[8,512]{1,0:T(8,128)S(1)} %dynamic-slice_bitcast_fusion.2, bf16[2048,8,64]{0,2,1:T(8,128)(2,1)S(1)} %get-tuple-element.511, bf16[2048,8,64]{0,2,1:T(8,128)(2,1)} %get-tuple-element.509, ...), kind=kOutput, calls=%fused_computation.21.clone.1 | convolution fusion | flops 1115680768 | bytes 70811648 | tf_op jit(solution)/shard_map/while/body/eval_jaxpr/qhd,khd->hqk/dot_general | solution.py:172
  890.1 27.4 %multiply_convert_fusion.3 = bf16[8,512,2048]{2,1,0:T(8,128)(2,1)} fusion(f32[8,512,2048]{2,1,0:T(8,128)} %get-tuple-element.441, f32[8,512,2048]{2,1,0:T(8,128)} %fusion.163, f32[8,512]{1,0:T(8,128)S(1)} %get-tuple-element.442), kind=kLoop, calls=%fused_computation.20.clone.1 | loop fusion | flops 25165824 | bytes 83902464 | tf_op jit(solution)/shard_map/while/body/eval_jaxpr/convert_element_type | solution.py:229
  917.5 8.7 fusion.165
  927.3 21.0 %dynamic_update_slice.44 = f32[4,512,8,64]{1,0,3,2:T(4,128)} dynamic-update-slice(f32[4,512,8,64]{1,0,3,2:T(4,128)} %get-tuple-element.493, f32[1,512,8,64]{1,0,3,2:T(1,128)S(1)} %copy.103, s32[]{:T(128)} %get-tuple-element.490, s32[]{:T(128)} %constant.84.clone.1..sunk.1, s32[]{:T(128)} %constant.84.clone.1..sunk.1, s32[]{:T(128)} %constant.84.clone.1..sunk.1) | dynamic-update-slice | bytes 2097156 | tf_op jit(solution)/shard_map/while/body/jit(dynamic_update_index_in_dim)/dynamic_update_slice | solution.py:250
  948.3 12.2 bitcast_add_fusion.4
  960.6 17.1 bitcast_add_fusion.5
  982.1 17.5 fusion.163
  1000.3 26.4 %multiply_reduce_fusion.2 = (f32[8,512]{1,0:T(8,128)S(1)}, f32[8,512,2048]{2,1,0:T(8,128)}) fusion(f32[8,512,2048]{2,1,0:T(8,128)} %fusion.163, f32[8,512]{1,0:T(8,128)S(1)} %dynamic-slice_bitcast_fusion.2, bf16[2048,8,64]{0,2,1:T(8,128)(2,1)S(1)} %get-tuple-element.511, bf16[2048,8,64]{0,2,1:T(8,128)(2,1)} %get-tuple-element.509, ...), kind=kOutput, calls=%fused_computation.21.clone.1 | convolution fusion | flops 1115680768 | bytes 70811648 | tf_op jit(solution)/shard_map/while/body/eval_jaxpr/qhd,khd->hqk/dot_general | solution.py:172
  1026.7 27.4 %multiply_convert_fusion.3 = bf16[8,512,2048]{2,1,0:T(8,128)(2,1)} fusion(f32[8,512,2048]{2,1,0:T(8,128)} %get-tuple-element.441, f32[8,512,2048]{2,1,0:T(8,128)} %fusion.163, f32[8,512]{1,0:T(8,128)S(1)} %get-tuple-element.442), kind=kLoop, calls=%fused_computation.20.clone.1 | loop fusion | flops 25165824 | bytes 83902464 | tf_op jit(solution)/shard_map/while/body/eval_jaxpr/convert_element_type | solution.py:229
  1054.1 8.7 fusion.165
  1063.9 21.0 %dynamic_update_slice.44 = f32[4,512,8,64]{1,0,3,2:T(4,128)} dynamic-update-slice(f32[4,512,8,64]{1,0,3,2:T(4,128)} %get-tuple-element.493, f32[1,512,8,64]{1,0,3,2:T(1,128)S(1)} %copy.103, s32[]{:T(128)} %get-tuple-element.490, s32[]{:T(128)} %constant.84.clone.1..sunk.1, s32[]{:T(128)} %constant.84.clone.1..sunk.1, s32[]{:T(128)} %constant.84.clone.1..sunk.1) | dynamic-update-slice | bytes 2097156 | tf_op jit(solution)/shard_map/while/body/jit(dynamic_update_index_in_dim)/dynamic_update_slice | solution.py:250
  1084.9 12.2 bitcast_add_fusion.4
  1097.1 17.0 bitcast_add_fusion.5
  1118.7 17.5 fusion.163
  1136.9 26.3 %multiply_reduce_fusion.2 = (f32[8,512]{1,0:T(8,128)S(1)}, f32[8,512,2048]{2,1,0:T(8,128)}) fusion(f32[8,512,2048]{2,1,0:T(8,128)} %fusion.163, f32[8,512]{1,0:T(8,128)S(1)} %dynamic-slice_bitcast_fusion.2, bf16[2048,8,64]{0,2,1:T(8,128)(2,1)S(1)} %get-tuple-element.511, bf16[2048,8,64]{0,2,1:T(8,128)(2,1)} %get-tuple-element.509, ...), kind=kOutput, calls=%fused_computation.21.clone.1 | convolution fusion | flops 1115680768 | bytes 70811648 | tf_op jit(solution)/shard_map/while/body/eval_jaxpr/qhd,khd->hqk/dot_general | solution.py:172
  1163.2 27.4 %multiply_convert_fusion.3 = bf16[8,512,2048]{2,1,0:T(8,128)(2,1)} fusion(f32[8,512,2048]{2,1,0:T(8,128)} %get-tuple-element.441, f32[8,512,2048]{2,1,0:T(8,128)} %fusion.163, f32[8,512]{1,0:T(8,128)S(1)} %get-tuple-element.442), kind=kLoop, calls=%fused_computation.20.clone.1 | loop fusion | flops 25165824 | bytes 83902464 | tf_op jit(solution)/shard_map/while/body/eval_jaxpr/convert_element_type | solution.py:229
  1190.6 8.7 fusion.165
  1200.4 21.0 %dynamic_update_slice.44 = f32[4,512,8,64]{1,0,3,2:T(4,128)} dynamic-update-slice(f32[4,512,8,64]{1,0,3,2:T(4,128)} %get-tuple-element.493, f32[1,512,8,64]{1,0,3,2:T(1,128)S(1)} %copy.103, s32[]{:T(128)} %get-tuple-element.490, s32[]{:T(128)} %constant.84.clone.1..sunk.1, s32[]{:T(128)} %constant.84.clone.1..sunk.1, s32[]{:T(128)} %constant.84.clone.1..sunk.1) | dynamic-update-slice | bytes 2097156 | tf_op jit(solution)/shard_map/while/body/jit(dynamic_update_index_in_dim)/dynamic_update_slice | solution.py:250
  1221.4 12.2 bitcast_add_fusion.4
  1233.6 17.0 bitcast_add_fusion.5
  1284.6 28.1 %convert_reduce_fusion = (f32[2048]{0:T(1024)}, bf16[2048,2048]{1,0:T(8,128)(2,1)}) fusion(f32[2048,2048]{1,0:T(8,128)} %get-tuple-element.277, bf16[2048,1024]{1,0:T(8,128)(2,1)} %all-gather.24.cloned.1.call-done, bf16[1024,2048]{1,0:T(8,128)(2,1)} %all-gather.22.cloned.1.call-done, f32[2048,2048]{1,0:T(8,128)} %get-tuple-element.313, f32[2048]{0:T(1024)S(1)} %copy-done.55), kind=kOutput, calls=%fused_computation.44 | convolution fusion | flops 8661235712 | bytes 50348032 | tf_op jit(solution)/shard_map/dot_general | solution.py:209
  1312.8 15.8 fusion.65
  1329.8 7.4 fusion.85
  1343.0 11.4 fusion.83
  1354.4 13.5 fusion.72
  1367.9 11.2 fusion.52
  1386.3 12.9 fusion.82
  1418.5 39.9 %reduce-scatter.20.cloned.1.call-done = f32[64,512]{1,0:T(8,128)} async-done(((f32[1024,512]{1,0:T(8,128)}), f32[64,512]{1,0:T(8,128)}) %reduce-scatter.20.cloned.1.call-update) | async-done | bytes 131088 | tf_op jit(solution)/shard_map/reduce_scatter | solution.py:316
  1461.1 104.8 %reduce-scatter.24.cloned.1.call-done = f32[64,2048]{1,0:T(8,128)} async-done(((f32[1024,2048]{1,0:T(8,128)}), f32[64,2048]{1,0:T(8,128)}) %reduce-scatter.24.cloned.1.call-update) | async-done | bytes 524304 | tf_op jit(solution)/shard_map/reduce_scatter | solution.py:318
  1568.5 98.6 %reduce-scatter.14.cloned.1.call-done = f32[1024,1024]{1,0:T(8,128)} async-done(((f32[2048,1024]{1,0:T(8,128)}), f32[1024,1024]{1,0:T(8,128)}) %reduce-scatter.14.cloned.1.call-update) | async-done | bytes 4194320 | tf_op jit(solution)/shard_map/reduce_scatter | solution.py:280
  1674.8 93.8 %reduce-scatter.12.cloned.1.call-done = f32[1024,1024]{1,0:T(8,128)} async-done(((f32[2048,1024]{1,0:T(8,128)}), f32[1024,1024]{1,0:T(8,128)}) %reduce-scatter.12.cloned.1.call-update) | async-done | bytes 4194320 | tf_op jit(solution)/shard_map/reduce_scatter | solution.py:195
  1773.0 54.9 %reduce-scatter.28.cloned.1.call-done = f32[64,13]{1,0:T(8,128)} async-done(((f32[1024,13]{1,0:T(8,128)}), f32[64,13]{1,0:T(8,128)}) %reduce-scatter.28.cloned.1.call-update) | async-done | bytes 3344
  (302 shorter events, 190.5 us)
Async XLA Ops:
  7.2 61.9 %all-gather.10.cloned.1.call-start = ((), (), s32[]{:S(2)}) async-start(), calls=%async_computation.9 | async-start | bytes 6291456 | tf_op jit(solution)/shard_map/all_gather | solution.py:141
  7.9 101.8 %all-gather.14.cloned.1.call-start = ((), (), s32[]{:S(2)}) async-start(), calls=%async_computation.11 | async-start | bytes 1114112 | tf_op jit(solution)/shard_map/all_gather | solution.py:111
  9.5 139.8 %all-gather.12.cloned.1.call-start = ((), (), s32[]{:S(2)}) async-start(), calls=%async_computation.10 | async-start | bytes 1114112 | tf_op jit(solution)/shard_map/all_gather | solution.py:110
  11.2 177.7 %all-gather.16.cloned.1.call-start = ((), (), s32[]{:S(2)}) async-start(), calls=%async_computation.12 | async-start | bytes 1114112 | tf_op jit(solution)/shard_map/all_gather | solution.py:112
  12.8 392.8 %all-gather.24.cloned.1.call-start = ((), (), s32[]{:S(2)}) async-start(), calls=%async_computation.17 | async-start | bytes 6291456 | tf_op jit(solution)/shard_map/all_gather | solution.py:206
  13.4 459.6 %reduce-scatter.22.cloned.1.call-start = ((), (), s32[]{:S(2)}) async-start(), calls=%async_computation.22 | async-start | bytes 2228224 | tf_op jit(solution)/shard_map/reduce_scatter | solution.py:317
  38.1 40.0 %copy-start.41 = (f32[1024,1]{0,1:T(1,128)}, f32[1024,1]{0,1:T(1,128)S(1)}, u32[]{:S(2)}) copy-start(f32[1024,1]{0,1:T(1,128)S(1)} %get-tuple-element.308) | copy-start | bytes 12292
  40.0 114.8 %copy-start.21 = (f32[2048,8]{0,1:T(8,128)}, f32[2048,8]{0,1:T(8,128)S(1)}, u32[]{:S(2)}) copy-start(f32[2048,8]{0,1:T(8,128)S(1)} %get-tuple-element.309) | copy-start | bytes 196612
  40.0 114.8 %copy-start.23 = (f32[2048,8]{0,1:T(8,128)}, f32[2048,8]{0,1:T(8,128)S(1)}, u32[]{:S(2)}) copy-start(f32[2048,8]{0,1:T(8,128)S(1)} %get-tuple-element.310) | copy-start | bytes 196612
  72.0 42.8 %copy-start.31 = (f32[2048]{0:T(1024)}, f32[2048]{0:T(1024)S(1)}, u32[]{:S(2)}) copy-start(f32[2048]{0:T(1024)S(1)} %broadcast_multiply_fusion) | copy-start | bytes 24580
  75.0 39.8 %copy-start.43 = (f32[2048]{0:T(1024)}, f32[2048]{0:T(1024)S(1)}, u32[]{:S(2)}) copy-start(f32[2048]{0:T(1024)S(1)} %fusion.53) | copy-start | bytes 24580
  75.0 39.8 %copy-start.35 = (f32[2048]{0:T(1024)}, f32[2048]{0:T(1024)S(1)}, u32[]{:S(2)}) copy-start(f32[2048]{0:T(1024)S(1)} %fusion.64) | copy-start | bytes 24580
  399.6 12.6 copy-start
  399.6 12.6 copy-start.17
  399.6 12.6 copy-start.62
  405.6 67.4 %copy-start.38 = (f32[64,512]{1,0:T(8,128)S(1)}, f32[64,512]{1,0:T(8,128)}, u32[]{:S(2)}) copy-start(f32[64,512]{1,0:T(8,128)} %param.36) | copy-start | bytes 393220
  405.6 67.4 %copy-start.39 = (f32[64,512]{1,0:T(8,128)S(1)}, f32[64,512]{1,0:T(8,128)}, u32[]{:S(2)}) copy-start(f32[64,512]{1,0:T(8,128)} %param.50) | copy-start | bytes 393220
  405.6 67.4 %copy-start.40 = (f32[64,512]{1,0:T(8,128)S(1)}, f32[64,512]{1,0:T(8,128)}, u32[]{:S(2)}) copy-start(f32[64,512]{1,0:T(8,128)} %param.43) | copy-start | bytes 393220
  405.6 119.9 %copy-start.32 = (f32[2048]{0:T(1024)S(1)}, f32[2048]{0:T(1024)}, u32[]{:S(2)}) copy-start(f32[2048]{0:T(1024)} %copy-done.31) | copy-start | bytes 24580
  405.6 119.9 %copy-start.36 = (f32[2048]{0:T(1024)S(1)}, f32[2048]{0:T(1024)}, u32[]{:S(2)}) copy-start(f32[2048]{0:T(1024)} %copy-done.35) | copy-start | bytes 24580
  405.6 119.9 %copy-start.45 = (f32[1024,1]{0,1:T(1,128)S(1)}, f32[1024,1]{0,1:T(1,128)}, u32[]{:S(2)}) copy-start(f32[1024,1]{0,1:T(1,128)} %get-tuple-element.303) | copy-start | bytes 12292
  405.6 119.9 %copy-start.56 = (f32[1024,1]{0,1:T(1,128)S(1)}, f32[1024,1]{0,1:T(1,128)}, u32[]{:S(2)}) copy-start(f32[1024,1]{0,1:T(1,128)} %get-tuple-element.302) | copy-start | bytes 12292
  412.3 113.2 %all-gather.20.cloned.1.call-start = ((), (), s32[]{:S(2)}) async-start(), calls=%async_computation.14 | async-start | bytes 4456448 | tf_op jit(solution)/shard_map/all_gather | solution.py:114
  413.1 187.1 %all-gather.18.cloned.1.call-start = ((), (), s32[]{:S(2)}) async-start(), calls=%async_computation.13 | async-start | bytes 1114112 | tf_op jit(solution)/shard_map/all_gather | solution.py:113
  414.0 171.5 %copy-start.54 = (f32[2048]{0:T(1024)}, f32[2048]{0:T(1024)S(1)}, u32[]{:S(2)}) copy-start(f32[2048]{0:T(1024)S(1)} %dynamic_slice.41) | copy-start | bytes 24580
  474.7 228.7 %reduce-scatter.26.cloned.1.call-start = ((), (), s32[]{:S(2)}) async-start(), calls=%async_computation.24 | async-start | bytes 8912896 | tf_op jit(solution)/shard_map/reduce_scatter | solution.py:319
  525.6 63.2 %copy-start.58 = (bf16[2048,1024]{1,0:T(8,128)(2,1)S(1)}, bf16[2048,1024]{1,0:T(8,128)(2,1)}, u32[]{:S(2)}) copy-start(bf16[2048,1024]{1,0:T(8,128)(2,1)} %all-gather.24.cloned.1.call-done) | copy-start | bytes 12582916
  600.1 684.5 %all-gather.22.cloned.1.call-start = ((), (), s32[]{:S(2)}) async-start(), calls=%async_computation.15 | async-start | bytes 4456448 | tf_op jit(solution)/shard_map/all_gather | solution.py:115
  600.2 103.3 %copy-start.25 = (f32[64,2048]{1,0:T(8,128)S(1)}, f32[64,2048]{1,0:T(8,128)}, u32[]{:S(2)}) copy-start(f32[64,2048]{1,0:T(8,128)} %param.38) | copy-start | bytes 1572868
  600.2 103.3 %copy-start.26 = (f32[64,2048]{1,0:T(8,128)S(1)}, f32[64,2048]{1,0:T(8,128)}, u32[]{:S(2)}) copy-start(f32[64,2048]{1,0:T(8,128)} %param.52) | copy-start | bytes 1572868
  600.2 106.0 %copy-start.1 = (bf16[2048,8,64]{0,2,1:T(8,128)(2,1)S(1)}, bf16[2048,8,64]{0,2,1:T(8,128)(2,1)}, u32[]{:S(2)}) copy-start(bf16[2048,8,64]{0,2,1:T(8,128)(2,1)} %copy-done) | copy-start | bytes 6291460
  600.2 106.0 %copy-start.18 = (s32[2048]{0:T(1024)S(1)}, s32[2048]{0:T(1024)}, u32[]{:S(2)}) copy-start(s32[2048]{0:T(1024)} %copy-done.17) | copy-start | bytes 24580
  600.2 106.0 %copy-start.63 = (s32[4]{0:T(128)S(1)}, s32[4]{0:T(128)}, u32[]{:S(2)}) copy-start(s32[4]{0:T(128)} %copy-done.62) | copy-start | bytes 52
  706.2 708.6 %reduce-scatter.18.cloned.1.call-start = ((), (), s32[]{:S(2)}) async-start(), calls=%async_computation.20 | async-start | bytes 2228224 | tf_op jit(solution)/shard_map/reduce_scatter | solution.py:315
  1267.8 148.8 %reduce-scatter.16.cloned.1.call-start = ((), (), s32[]{:S(2)}) async-start(), calls=%async_computation.19 | async-start | bytes 2228224 | tf_op jit(solution)/shard_map/reduce_scatter | solution.py:314
  1275.2 183.2 %reduce-scatter.20.cloned.1.call-start = ((), (), s32[]{:S(2)}) async-start(), calls=%async_computation.21 | async-start | bytes 2228224 | tf_op jit(solution)/shard_map/reduce_scatter | solution.py:316
  1284.5 281.5 %reduce-scatter.24.cloned.1.call-start = ((), (), s32[]{:S(2)}) async-start(), calls=%async_computation.23 | async-start | bytes 8912896 | tf_op jit(solution)/shard_map/reduce_scatter | solution.py:318
  1284.6 28.2 %copy-start.33 = (f32[2048]{0:T(1024)S(1)}, f32[2048]{0:T(1024)}, u32[]{:S(2)}) copy-start(f32[2048]{0:T(1024)} %copy-done.31) | copy-start | bytes 24580
  1284.6 28.2 %copy-start.37 = (f32[2048]{0:T(1024)S(1)}, f32[2048]{0:T(1024)}, u32[]{:S(2)}) copy-start(f32[2048]{0:T(1024)} %copy-done.35) | copy-start | bytes 24580
  1284.6 28.2 %copy-start.46 = (f32[1024,1]{0,1:T(1,128)S(1)}, f32[1024,1]{0,1:T(1,128)}, u32[]{:S(2)}) copy-start(f32[1024,1]{0,1:T(1,128)} %get-tuple-element.303) | copy-start | bytes 12292
  1284.6 28.2 %copy-start.57 = (f32[1024,1]{0,1:T(1,128)S(1)}, f32[1024,1]{0,1:T(1,128)}, u32[]{:S(2)}) copy-start(f32[1024,1]{0,1:T(1,128)} %get-tuple-element.302) | copy-start | bytes 12292
  1328.6 338.5 %reduce-scatter.14.cloned.1.call-start = ((), (), s32[]{:S(2)}) async-start(), calls=%async_computation.18 | async-start | bytes 12582912 | tf_op jit(solution)/shard_map/reduce_scatter | solution.py:280
  1329.8 13.2 slice-start.1
  1343.0 11.4 copy-start.3
  1343.0 11.4 copy-start.19
  1343.0 11.4 copy-start.42
  1354.4 13.5 copy-start.44
  1367.9 11.2 copy-start.4
  1386.2 13.0 copy-start.6
  1386.2 13.0 copy-start.20
  1386.2 382.4 %reduce-scatter.12.cloned.1.call-start = ((), (), s32[]{:S(2)}) async-start(), calls=%async_computation.16 | async-start | bytes 12582912 | tf_op jit(solution)/shard_map/reduce_scatter | solution.py:195
  1404.9 11.8 copy-start.29
  1404.9 53.5 %copy-start.30 = (f32[64,512]{1,0:T(8,128)S(1)}, f32[64,512]{1,0:T(8,128)}, u32[]{:S(2)}) copy-start(f32[64,512]{1,0:T(8,128)} %param.35) | copy-start | bytes 393220
  1404.9 161.0 %copy-start.12 = (f32[64,2048]{1,0:T(8,128)S(1)}, f32[64,2048]{1,0:T(8,128)}, u32[]{:S(2)}) copy-start(f32[64,2048]{1,0:T(8,128)} %param.37) | copy-start | bytes 1572868
  1404.9 161.0 %copy-start.27 = (f32[64,2048]{1,0:T(8,128)S(1)}, f32[64,2048]{1,0:T(8,128)}, u32[]{:S(2)}) copy-start(f32[64,2048]{1,0:T(8,128)} %param.51) | copy-start | bytes 1572868
  1405.0 363.7 %copy-start.7 = (bf16[1024,1024]{1,0:T(8,128)(2,1)S(1)}, bf16[1024,1024]{1,0:T(8,128)(2,1)}, u32[]{:S(2)}) copy-start(bf16[1024,1024]{1,0:T(8,128)(2,1)} %param.29) | copy-start | bytes 6291460
  1405.0 363.7 %copy-start.48 = (f32[1024,1]{0,1:T(1,128)S(1)}, f32[1024,1]{0,1:T(1,128)}, u32[]{:S(2)}) copy-start(f32[1024,1]{0,1:T(1,128)} %get-tuple-element.300) | copy-start | bytes 12292
  1405.0 363.7 %copy-start.49 = (f32[1024,1]{0,1:T(1,128)S(1)}, f32[1024,1]{0,1:T(1,128)}, u32[]{:S(2)}) copy-start(f32[1024,1]{0,1:T(1,128)} %get-tuple-element.301) | copy-start | bytes 12292
  1405.0 422.9 %reduce-scatter.28.cloned.1.call-start = ((), (), s32[]{:S(2)}) async-start(), calls=%async_computation.25 | async-start | bytes 557056
  1416.7 255.6 %copy-start.50 = (f32[1024]{0:T(1024)S(1)}, f32[1024]{0:T(1024)}, u32[]{:S(2)}) copy-start(f32[1024]{0:T(1024)} %get-tuple-element.196) | copy-start | bytes 12292
  1416.7 255.6 %copy-start.51 = (f32[1024]{0:T(1024)S(1)}, f32[1024]{0:T(1024)}, u32[]{:S(2)}) copy-start(f32[1024]{0:T(1024)} %get-tuple-element.205) | copy-start | bytes 12292
  1568.5 265.2 %copy-start.47 = (f32[64,13]{0,1:T(8,128)S(1)}, f32[64,13]{0,1:T(8,128)}, u32[]{:S(2)}) copy-start(f32[64,13]{0,1:T(8,128)} %param.39) | copy-start | bytes 9988
  1568.5 265.2 %copy-start.52 = (f32[64,13]{0,1:T(8,128)S(1)}, f32[64,13]{0,1:T(8,128)}, u32[]{:S(2)}) copy-start(f32[64,13]{0,1:T(8,128)} %param.53) | copy-start | bytes 9988
  1568.5 265.2 %copy-start.53 = (f32[64,13]{0,1:T(8,128)S(1)}, f32[64,13]{0,1:T(8,128)}, u32[]{:S(2)}) copy-start(f32[64,13]{0,1:T(8,128)} %param.46) | copy-start | bytes 9988
  (21 other events, 116.0 us)
Sparse Core Ops, SparseCore 0:
  9.6 59.4 all-gather.9
  71.8 37.9 all-gather.13
  112.5 36.8 all-gather.11
  152.0 36.8 all-gather.15
  190.3 55.6 all-gather.23
  412.4 60.4 reduce-scatter.21
  475.9 49.5 all-gather.19
  528.5 36.4 all-gather.17
  600.2 103.2 reduce-scatter.25
  706.3 50.4 all-gather.21
  1268.0 61.3 reduce-scatter.17
  1332.9 60.6 reduce-scatter.15
  1397.8 60.5 reduce-scatter.19
  1462.3 103.5 reduce-scatter.23
  1568.1 99.0 reduce-scatter.13
  1669.4 99.2 reduce-scatter.11
  1772.1 55.7 reduce-scatter.27
where the time goes:
time: 1850 us; the launch traced here: 1840 us
  waiting for transfers between devices  723 us (39%)
  matrix products  664 us (36%)
  other arithmetic  257 us (14%)
  local copies, waits for them, and re-layouts  137 us (7%)
  blocking collectives  28.2 us (2%)
    dot_general x8, matrix products, masked_scores(): jnp.einsum('qhd,khd->hqk', query_block, key_rows, preferred_element_type=...  167 us
    convert_element_type x4, other arithmetic, backward_block(): grad_scores = (probs * (grad_probs - centre)).astype(jnp.bfloat16)  110 us
    reduce_scatter x1, waiting for transfers between devices, shards(): lax.psum_scatter(grad_in, 'dp', scatter_dimension=0, tiled=True)  105 us
    reduce_scatter x1, waiting for transfers between devices, shards(): lax.psum_scatter(grad_rows_part, 'tensor', scatter_dimension=0, tiled=True)  98.6 us
    reduce_scatter x1, waiting for transfers between devices, shards(): lax.psum_scatter(grad_out, 'dp', scatter_dimension=0, tiled=True)  96.8 us
    reduce_scatter x1, waiting for transfers between devices, shards(): lax.psum_scatter(mixed, 'tensor', scatter_dimension=0, tiled=True)  93.8 us
    dynamic_update_slice x8, local copies, waits for them, and re-layouts, shards(): lax.scan(backward_block, (zero_heads, zero_heads), (starts, log_totals))  88.4 us
    dot_general x4, matrix products, backward_block(): jnp.einsum('qhd,khd->hqk', grad_block, value_rows, preferred_element_type...  70.1 us
  transfers between devices with their start and end apart: 17, of which 12 were waited for; matrix products, arithmetic and copies ran while one was open for 56% of the time, Pallas kernels for 0%

commit v1 on v0

v1 whole, which is shorter than its diff:
```python
import jax
import jax.numpy as jnp
from jax import lax
from jax.experimental import pallas as pl
from jax.experimental.pallas import tpu as pltpu
from jax.sharding import PartitionSpec as P

HEAD_DIM = 64
ROT = 16
STEP = 10


NORM_EPS = 1e-05
BETA_FIRST = 0.9
BETA_SECOND = 0.95
ADAM_EPS = 1e-08
WEIGHT_DECAY = 0.01
RATE_MATRIX = 0.04
RATE_DENSE = 0.2
RATE_VECTOR = 0.5
MASKED = -1000000000.0


def layout(lengths, offsets, total_rows):
    row_ids = jnp.arange(total_rows, dtype=jnp.int32)
    inside = (
        (row_ids[:, None] >= offsets[None, :])
        & (row_ids[:, None] < offsets[None, :] + lengths[None, :])
    ).astype(jnp.int32)
    slot_ids = jnp.arange(lengths.shape[0], dtype=jnp.int32)
    member = jnp.sum(inside, axis=1)
    segment = jnp.where(
        member > 0, jnp.sum(inside * slot_ids[None, :], axis=1), lengths.shape[0] + row_ids
    )
    position = jnp.where(member > 0, row_ids - jnp.sum(inside * offsets[None, :], axis=1), 0)
    return (segment, position)


LANES = 128
Q_BLOCK = 256
K_BLOCK = 512
INV_SQRT2 = 0.7071067811865476
INV_SQRT_2PI = 0.3989422804014327


def dot_nn(left, right):
    return lax.dot_general(
        left, right, (((1,), (0,)), ((), ())), preferred_element_type=jnp.float32
    )


def dot_nt(left, right):
    return lax.dot_general(
        left, right, (((1,), (1,)), ((), ())), preferred_element_type=jnp.float32
    )


def dot_tn(left, right):
    return lax.dot_general(
        left, right, (((0,), (0,)), ((), ())), preferred_element_type=jnp.float32
    )


def rotary_tables(position):
    half = ROT // 2
    lane = jnp.arange(LANES, dtype=jnp.int32) % HEAD_DIM
    freq = 10000.0 ** (-2.0 * (lane % half).astype(jnp.float32) / ROT)
    angle = position.astype(jnp.float32)[:, None] * freq[None, :]
    cosine, sine = jnp.cos(angle), jnp.sin(angle)
    return (
        jnp.where(lane < ROT, cosine, 1.0),
        jnp.where(lane < half, -sine, 0.0),
        jnp.where((lane >= half) & (lane < ROT), sine, 0.0),
    )


def turn(values, keep, ahead, behind):
    half = ROT // 2
    return (
        values * keep
        + pltpu.roll(values, LANES - half, 1) * ahead
        + pltpu.roll(values, half, 1) * behind
    )


def attention_kernel(
    first_ref, q_ref, k_ref, v_ref, do_ref, qkeep_ref, qahead_ref, qback_ref,
    keep_ref, ahead_ref, back_ref,
    out_ref, gq_ref, gk_ref, gv_ref,
    k_low, v_low, scores, pulls, gk_sum, gv_sum,
):
    block = pl.program_id(1)
    rows = k_ref.shape[0]
    q_rows = q_ref.shape[0]
    k_rows = min(K_BLOCK, rows)
    scale = HEAD_DIM ** (-0.5)

    @pl.when(block == 0)
    def _():
        k_low[...] = turn(
            k_ref[...], keep_ref[...], ahead_ref[...], back_ref[...]
        ).astype(jnp.bfloat16)
        v_low[...] = v_ref[...].astype(jnp.bfloat16)
        gk_sum[...] = jnp.zeros_like(gk_sum)
        gv_sum[...] = jnp.zeros_like(gv_sum)

    lane = lax.broadcasted_iota(jnp.int32, (q_rows, LANES), 1)
    q_low = turn(q_ref[...], qkeep_ref[...], qahead_ref[...], qback_ref[...])
    q_low = q_low.astype(jnp.bfloat16).astype(jnp.float32) * scale
    do_low = do_ref[...].astype(jnp.float32)
    mine = (lane < HEAD_DIM, lane >= HEAD_DIM)
    q_of = [jnp.where(m, q_low, 0.0).astype(jnp.bfloat16) for m in mine]
    do_of = [jnp.where(m, do_low, 0.0).astype(jnp.bfloat16) for m in mine]
    q_both = jnp.concatenate(q_of, axis=0)
    do_both = jnp.concatenate(do_of, axis=0)
    first = first_ref[...]
    row_id = block * q_rows + lax.broadcasted_iota(jnp.int32, (1, q_rows), 1)
    chunks = (block * q_rows + q_rows + k_rows - 1) // k_rows

    def at(chunk):
        return pl.ds(pl.multiple_of(chunk * k_rows, k_rows), k_rows)

    def score_step(chunk, tops):
        key_id = chunk * k_rows + lax.broadcasted_iota(jnp.int32, (k_rows, q_rows), 0)
        allowed = (key_id >= first) & (key_id <= row_id)
        new = []
        for h in range(2):
            block_scores = jnp.where(allowed, dot_nt(k_low[at(chunk), :], q_of[h]), MASKED)
            scores[h, at(chunk), :] = block_scores
            new.append(jnp.maximum(tops[h], jnp.max(block_scores, axis=0, keepdims=True)))
        return tuple(new)

    low_row = jnp.full((1, q_rows), MASKED, jnp.float32)
    tops = lax.fori_loop(0, chunks, score_step, (low_row, low_row))

    def weight_step(chunk, sums):
        new = []
        for h in range(2):
            exps = jnp.exp(scores[h, at(chunk), :] - tops[h])
            pull = dot_nt(v_low[at(chunk), :], do_of[h])
            scores[h, at(chunk), :] = exps
            pulls[h, at(chunk), :] = pull
            new.append(sums[2 * h] + jnp.sum(exps, axis=0, keepdims=True))
            new.append(sums[2 * h + 1] + jnp.sum(exps * pull, axis=0, keepdims=True))
        return tuple(new)

    zero_row = jnp.zeros((1, q_rows), jnp.float32)
    sums = lax.fori_loop(0, chunks, weight_step, (zero_row,) * 4)
    shares = [1.0 / sums[2 * h] for h in range(2)]
    centres = [sums[2 * h + 1] * shares[h] for h in range(2)]

    def gradient_step(chunk, carry):
        new = []
        lows, grads = [], []
        for h in range(2):
            probs = scores[h, at(chunk), :] * shares[h]
            lows.append(probs.astype(jnp.bfloat16))
            grads.append((probs * (pulls[h, at(chunk), :] - centres[h])).astype(jnp.bfloat16))
            new.append(carry[2 * h] + dot_tn(v_low[at(chunk), :], lows[h]))
            new.append(carry[2 * h + 1] + dot_tn(k_low[at(chunk), :], grads[h]))
        gv_sum[at(chunk), :] += dot_nn(jnp.concatenate(lows, axis=1), do_both)
        gk_sum[at(chunk), :] += dot_nn(jnp.concatenate(grads, axis=1), q_both)
        return tuple(new)

    zero_block = jnp.zeros((LANES, q_rows), jnp.float32)
    out_one, gq_one, out_two, gq_two = lax.fori_loop(
        0, chunks, gradient_step, (zero_block,) * 4
    )
    upper = lax.broadcasted_iota(jnp.int32, (LANES, q_rows), 0) < HEAD_DIM
    out_ref[...] = jnp.where(upper, out_one, out_two).T.astype(jnp.bfloat16)
    gq = jnp.where(upper, gq_one, gq_two).T * scale
    gq_ref[...] = turn(gq, qkeep_ref[...], -qahead_ref[...], -qback_ref[...]).astype(jnp.bfloat16)

    @pl.when(block == pl.num_programs(1) - 1)
    def _():
        gk_ref[...] = turn(
            gk_sum[...], keep_ref[...], -ahead_ref[...], -back_ref[...]
        ).astype(jnp.bfloat16)
        gv_ref[...] = gv_sum[...].astype(jnp.bfloat16)


def attention(first_row, lin, grad_attended, tables):
    rows, cols = grad_attended.shape
    pairs = cols // LANES
    q_rows = min(Q_BLOCK, rows)
    blocks = rows // q_rows
    tall = lambda shift: pl.BlockSpec((rows, LANES), lambda p, b: (0, p + shift))
    here = pl.BlockSpec((q_rows, LANES), lambda p, b: (b, p))
    table_here = pl.BlockSpec((q_rows, LANES), lambda p, b: (b, 0))
    table_tall = pl.BlockSpec((rows, LANES), lambda p, b: (0, 0))
    low = jax.ShapeDtypeStruct((rows, cols), jnp.bfloat16)
    return pl.pallas_call(
        attention_kernel,
        grid=(pairs, blocks),
        in_specs=[pl.BlockSpec((1, q_rows), lambda p, b: (0, b)), here, tall(pairs), tall(2 * pairs),
                  here] + [table_here] * 3 + [table_tall] * 3,
        out_specs=[here, here, tall(0), tall(0)],
        out_shape=[low] * 4,
        scratch_shapes=[
            pltpu.VMEM((rows, LANES), jnp.bfloat16),
            pltpu.VMEM((rows, LANES), jnp.bfloat16),
            pltpu.VMEM((2, rows, q_rows), jnp.float32),
            pltpu.VMEM((2, rows, q_rows), jnp.float32),
            pltpu.VMEM((rows, LANES), jnp.float32),
            pltpu.VMEM((rows, LANES), jnp.float32),
        ],
        compiler_params=pltpu.CompilerParams(vmem_limit_bytes=44 * 2**20),
        cost_estimate=pl.CostEstimate(
            flops=60 * 10**9, bytes_accessed=30 * 2**20, transcendentals=rows * rows * pairs
        ),
        name="attention",
    )(first_row[None, :], lin, lin, lin, grad_attended, *tables, *tables)


def hidden_kernel(normed_ref, dy_ref, in_ref, out_ref, bias_ref, act_ref, grad_ref):
    pre = dot_nn(normed_ref[...], in_ref[...]) + bias_ref[...]
    pull = dot_nn(dy_ref[...], out_ref[...])
    phi = 0.5 * (1.0 + lax.erf(pre * INV_SQRT2))
    act_ref[...] = (pre * phi).astype(jnp.bfloat16)
    slope = phi + pre * (INV_SQRT_2PI * jnp.exp(-0.5 * pre * pre))
    grad_ref[...] = (pull * slope).astype(jnp.bfloat16)


def hidden_units(normed, grad_rows, in_full, out_full, bias):
    rows, depth = normed.shape
    units = in_full.shape[1]
    tile_rows, tile_units = min(512, rows), min(512, units)
    row_spec = pl.BlockSpec((tile_rows, depth), lambda u, r: (r, 0))
    weight_spec = pl.BlockSpec((depth, tile_units), lambda u, r: (0, u))
    tile = pl.BlockSpec((tile_rows, tile_units), lambda u, r: (r, u))
    low = jax.ShapeDtypeStruct((rows, units), jnp.bfloat16)
    return pl.pallas_call(
        hidden_kernel,
        grid=(units // tile_units, rows // tile_rows),
        in_specs=[row_spec, row_spec, weight_spec, weight_spec,
                  pl.BlockSpec((1, tile_units), lambda u, r: (0, u))],
        out_specs=[tile, tile],
        out_shape=[low, low],
        compiler_params=pltpu.CompilerParams(vmem_limit_bytes=40 * 2**20),
        cost_estimate=pl.CostEstimate(
            flops=4 * rows * depth * units, bytes_accessed=40 * 2**20,
            transcendentals=2 * rows * units,
        ),
        name="hidden_units",
    )(normed, grad_rows, in_full, out_full, bias[None, :])


def adam_update(weight_matrix, grad, first, second, rate, decay):
    first = BETA_FIRST * first + (1.0 - BETA_FIRST) * grad
    second = BETA_SECOND * second + (1.0 - BETA_SECOND) * grad * grad
    fixed_first = first / (1.0 - BETA_FIRST**STEP)
    fixed_second = second / (1.0 - BETA_SECOND**STEP)
    weight_matrix = weight_matrix - rate * (
        fixed_first / (jnp.sqrt(fixed_second) + ADAM_EPS) + decay * weight_matrix
    )
    return (first, second, weight_matrix)


def shards(
    tokens,
    cotangent,
    sequence_lengths,
    sequence_starts,
    weight_query,
    weight_key,
    weight_value,
    weight_dense,
    weight_in,
    weight_out,
    vectors,
    first_query,
    first_key,
    first_value,
    first_dense,
    first_in,
    first_out,
    first_vectors,
    second_query,
    second_key,
    second_value,
    second_dense,
    second_in,
    second_out,
    second_vectors,
):
    tensor_size = lax.axis_size("tensor")
    tensor_rank = lax.axis_index("tensor")
    shard_rows, model_width = tokens.shape
    all_rows = shard_rows * tensor_size
    segment, position = layout(sequence_lengths[0], sequence_starts[0], all_rows)
    row_ids = jnp.arange(all_rows, dtype=jnp.int32)
    first_row = jnp.where(segment < sequence_lengths.shape[1], row_ids - position, row_ids)
    masters = (weight_query, weight_key, weight_value, weight_dense, weight_in, weight_out, vectors)
    low = jnp.bfloat16
    swap = [(0, 1), (1, 0)]

    def both_rows(mine):
        if tensor_size != 2:
            return lax.all_gather(mine, "tensor", axis=0, tiled=True)
        other = lax.ppermute(mine, "tensor", swap)
        rows = jnp.zeros((all_rows, model_width), mine.dtype)
        rows = lax.dynamic_update_slice(rows, mine, (tensor_rank * shard_rows, 0))
        return lax.dynamic_update_slice(rows, other, ((1 - tensor_rank) * shard_rows, 0))

    def summed_rows(part):
        if tensor_size != 2:
            return lax.psum_scatter(part, "tensor", scatter_dimension=0, tiled=True)
        mine = lax.dynamic_slice_in_dim(part, tensor_rank * shard_rows, shard_rows, 0)
        theirs = lax.dynamic_slice_in_dim(part, (1 - tensor_rank) * shard_rows, shard_rows, 0)
        return mine + lax.ppermute(theirs.astype(low), "tensor", swap).astype(jnp.float32)

    def gather(values):
        return lax.all_gather(values, "dp", axis=0, tiled=True)

    vector_copy = gather(vectors.astype(low)).astype(jnp.float32)
    in_full = gather(weight_in.astype(low))
    out_full = gather(weight_out.astype(low))
    attn_full = gather(
        jnp.concatenate([weight_query, weight_key, weight_value, weight_dense], axis=1).astype(low)
    )
    head_cols = weight_query.shape[1]
    hidden_cols = weight_in.shape[1]
    qkv_full = attn_full[:, : 3 * head_cols]
    dense_full = attn_full[:, 3 * head_cols :]
    gain_one, shift_one, gain_two, shift_two, bias_dense, bias_out = [
        vector_copy[:, column] for column in range(6)
    ]
    bias_qkv = lax.dynamic_slice_in_dim(
        vector_copy[:, 6:9].T, tensor_rank * head_cols, head_cols, axis=1
    ).reshape(-1)
    bias_in = lax.dynamic_slice_in_dim(
        vector_copy[:, 9:].T.reshape(-1), tensor_rank * hidden_cols, hidden_cols
    )
    whole_rows = both_rows(tokens).astype(jnp.float32)
    grad_rows = both_rows(cotangent)
    centred = whole_rows - jnp.mean(whole_rows, axis=-1, keepdims=True)
    rstd = lax.rsqrt(jnp.mean(centred * centred, axis=-1, keepdims=True) + NORM_EPS)
    unit = centred * rstd
    normed_one = (unit * gain_one + shift_one).astype(low)
    normed_two = (unit * gain_two + shift_two).astype(low)

    activated, grad_pre = hidden_units(normed_two, grad_rows, in_full, out_full, bias_in)
    grad_in = dot_tn(normed_two, grad_pre).astype(low)
    grad_out = dot_tn(grad_rows, activated).astype(low)

    def spread(values):
        return lax.psum_scatter(values, "dp", scatter_dimension=0, tiled=True)

    sum_in = spread(grad_in)
    sum_out = spread(grad_out)
    grad_two = dot_nt(grad_pre, in_full)

    lin = dot_nn(normed_one, qkv_full) + bias_qkv
    grad_attended = dot_nn(grad_rows, dense_full).astype(low)
    lin, grad_attended, grad_in, grad_out = lax.optimization_barrier(
        (lin, grad_attended, grad_in, grad_out)
    )
    attended, grad_query_lin, grad_key_lin, grad_value_lin = attention(
        first_row, lin, grad_attended, rotary_tables(position)
    )
    grad_qkv_lin = jnp.concatenate([grad_query_lin, grad_key_lin, grad_value_lin], axis=1)
    grad_qkv = dot_tn(normed_one, grad_qkv_lin).astype(low)
    sum_qkv = spread(grad_qkv)
    sum_dense = spread(dot_tn(grad_rows, attended).astype(low))
    mixed = dot_nt(attended, dense_full) + dot_nt(activated, out_full)
    output = (tokens.astype(jnp.float32) + summed_rows(mixed) + bias_dense + bias_out).astype(low)

    grad_one = dot_nt(grad_qkv_lin, qkv_full)
    pull = grad_one * gain_one + grad_two * gain_two
    grad_rows_part = rstd * (
        pull
        - jnp.mean(pull, axis=-1, keepdims=True)
        - unit * jnp.mean(pull * unit, axis=-1, keepdims=True)
    )
    input_grad = (cotangent.astype(jnp.float32) + summed_rows(grad_rows_part)).astype(low)

    def placed(values, total_len):
        return lax.dynamic_update_slice(
            jnp.zeros((total_len,), jnp.float32), values, (tensor_rank * values.shape[0],)
        )

    local_bias = jnp.sum(cotangent.astype(jnp.float32), axis=0)
    bias_grads = [
        placed(jnp.sum(part.astype(jnp.float32), axis=0), model_width)
        for part in (grad_query_lin, grad_key_lin, grad_value_lin)
    ]
    grad_bias_in = placed(jnp.sum(grad_pre.astype(jnp.float32), axis=0), hidden_cols * tensor_size)
    grad_vector = jnp.concatenate(
        [
            jnp.stack(
                [
                    jnp.sum(grad_one * unit, axis=0),
                    jnp.sum(grad_one, axis=0),
                    jnp.sum(grad_two * unit, axis=0),
                    jnp.sum(grad_two, axis=0),
                    local_bias,
                    local_bias,
                ]
                + bias_grads,
                axis=1,
            ),
            grad_bias_in.reshape(-1, model_width).T,
        ],
        axis=1,
    )
    vector_grad = lax.psum(spread(grad_vector), "tensor")
    sums = [sum_qkv[:, at * head_cols : (at + 1) * head_cols] for at in range(3)]
    grads = [part.astype(jnp.float32) for part in (*sums, sum_dense, sum_in, sum_out)]
    grads.append(vector_grad)
    firsts = (first_query, first_key, first_value, first_dense, first_in, first_out, first_vectors)
    seconds = (
        second_query,
        second_key,
        second_value,
        second_dense,
        second_in,
        second_out,
        second_vectors,
    )
    rates = (
        RATE_MATRIX,
        RATE_MATRIX,
        RATE_MATRIX,
        RATE_DENSE,
        RATE_MATRIX,
        RATE_MATRIX,
        RATE_VECTOR,
    )
    decays = (
        WEIGHT_DECAY,
        WEIGHT_DECAY,
        WEIGHT_DECAY,
        WEIGHT_DECAY,
        WEIGHT_DECAY,
        WEIGHT_DECAY,
        0.0,
    )
    updated = [
        adam_update(
            masters[slot], grads[slot], firsts[slot], seconds[slot], rates[slot], decays[slot]
        )
        for slot in range(7)
    ]
    return (
        output,
        input_grad,
        updated[0][0],
        updated[1][0],
        updated[2][0],
        updated[3][0],
        updated[4][0],
        updated[5][0],
        updated[6][0],
        updated[0][1],
        updated[1][1],
        updated[2][1],
        updated[3][1],
        updated[4][1],
        updated[5][1],
        updated[6][1],
        updated[0][2],
        updated[1][2],
        updated[2][2],
        updated[3][2],
        updated[4][2],
        updated[5][2],
        updated[6][2],
    )


def solution(mesh):
    in_specs = (
        P(("dp", "tensor"), None),
        P(("dp", "tensor"), None),
        P("dp", None),
        P("dp", None),
        P("dp", "tensor"),
        P("dp", "tensor"),
        P("dp", "tensor"),
        P("dp", "tensor"),
        P("dp", "tensor"),
        P("dp", "tensor"),
        P("dp", None),
        P("dp", "tensor"),
        P("dp", "tensor"),
        P("dp", "tensor"),
        P("dp", "tensor"),
        P("dp", "tensor"),
        P("dp", "tensor"),
        P("dp", None),
        P("dp", "tensor"),
        P("dp", "tensor"),
        P("dp", "tensor"),
        P("dp", "tensor"),
        P("dp", "tensor"),
        P("dp", "tensor"),
        P("dp", None),
    )
    out_specs = (
        P(("dp", "tensor"), None),
        P(("dp", "tensor"), None),
        P("dp", "tensor"),
        P("dp", "tensor"),
        P("dp", "tensor"),
        P("dp", "tensor"),
        P("dp", "tensor"),
        P("dp", "tensor"),
        P("dp", None),
        P("dp", "tensor"),
        P("dp", "tensor"),
        P("dp", "tensor"),
        P("dp", "tensor"),
        P("dp", "tensor"),
        P("dp", "tensor"),
        P("dp", None),
        P("dp", "tensor"),
        P("dp", "tensor"),
        P("dp", "tensor"),
        P("dp", "tensor"),
        P("dp", "tensor"),
        P("dp", "tensor"),
        P("dp", None),
    )
    return jax.shard_map(shards, mesh=mesh, in_specs=in_specs, out_specs=out_specs, check_vma=False)
```

time: 1850 us -> 721 us (0.39)
  matrix products: 664 us -> 106 us
  waiting for transfers between devices: 723 us -> 318 us
  other arithmetic: 257 us -> 54.7 us
  Pallas kernels: 0 us -> 151 us
  local copies, waits for them, and re-layouts: 137 us -> 33.9 us
    dot_general x46 -> x10, matrix products: 664 us -> 106 us  [the longest x4 46.7 us: dot_nt(): lax.dot_general(left, right, (((1,), (1,)), ((), ())), preferred_element_...]
    reduce_scatter x8 -> x4, waiting for transfers between devices: 493 us -> 183 us  [spread(): return lax.psum_scatter(values, 'dp', scatter_dimension=0, tiled=True)]
    all_gather x8 -> x3, waiting for transfers between devices: 174 us -> 2.12 us  [gather(): return lax.all_gather(values, 'dp', axis=0, tiled=True)]
    pallas_call x0 -> x2, Pallas kernels: none -> 151 us  [the longest x1 128 us: attention(): pl.pallas_call(attention_kernel, grid=(pairs, blocks), in_specs=[pl.Block...]
    ppermute x0 -> x4, waiting for transfers between devices: none -> 132 us  [the longest x2 79.2 us: summed_rows(): lax.ppermute(theirs.astype(low), 'tensor', swap).astype(jnp.float32)]
    convert_element_type x12 -> x6, other arithmetic: 122 us -> 12.4 us  [the longest x1 5.67 us: shards(): (tokens.astype(jnp.float32) + summed_rows(mixed) + bias_dense + bias_out)...]
    dynamic_update_slice x8 -> x4, local copies, waits for them, and re-layouts: 88.4 us -> 4.32 us  [the longest x2 3.78 us: both_rows(): lax.dynamic_update_slice(rows, other, ((1 - tensor_rank) * shard_rows, 0))]
    reduce_sum x10 -> x6, other arithmetic: 83.4 us -> 9.56 us  [the longest x1 4.73 us: shards(): jnp.sum(grad_pre.astype(jnp.float32), axis=0)]
  transfers between devices with their start and end apart: 17 -> 12, of which waited for: 12 -> 8; matrix products, arithmetic and copies ran while one was open for 56% -> 16% of each run, Pallas kernels for 0% -> 3%
where the time goes in v1:
time: 721 us; the launch traced here: 712 us
  waiting for transfers between devices  318 us (44%)
  Pallas kernels  151 us (21%)
  matrix products  106 us (15%)
  other arithmetic  54.7 us (8%)
  local copies, waits for them, and re-layouts  33.9 us (5%)
  blocking collectives  27.2 us (4%)
  between operations  15.1 us (2%)
    reduce_scatter x4, waiting for transfers between devices, spread(): return lax.psum_scatter(values, 'dp', scatter_dimension=0, tiled=True)  183 us
    pallas_call x1, Pallas kernels, attention(): pl.pallas_call(attention_kernel, grid=(pairs, blocks), in_specs=[pl.Block...  128 us
    ppermute x2, waiting for transfers between devices, summed_rows(): lax.ppermute(theirs.astype(low), 'tensor', swap).astype(jnp.float32)  79.2 us
    ppermute x2, waiting for transfers between devices, both_rows(): other = lax.ppermute(mine, 'tensor', swap)  52.4 us
    dot_general x4, matrix products, dot_nt(): lax.dot_general(left, right, (((1,), (1,)), ((), ())), preferred_element_...  46.7 us
    dot_general x4, matrix products, dot_tn(): lax.dot_general(left, right, (((0,), (0,)), ((), ())), preferred_element_...  42.7 us
    unnamed x86, local copies, waits for them, and re-layouts  23.9 us
    pallas_call x1, Pallas kernels, hidden_units(): pl.pallas_call(hidden_kernel, grid=(units // tile_units, rows // tile_row...  23.1 us
  transfers between devices with their start and end apart: 12, of which 8 were waited for; matrix products, arithmetic and copies ran while one was open for 16% of the time, Pallas kernels for 3%

profile of v1, /device:TPU:0, one launch (start us, length us, event | category | flops | bytes accessed | tf_op | source)
XLA Modules:
  0.0 712.5 jit_solution(13939030804840123410)
XLA Ops:
  7.3 1.9 convert_element_type.117
  9.3 1.8 convert_element_type.118
  11.1 3.0 collective-permute-start
  14.2 0.9 convert.12
  15.1 0.9 convert.13
  16.1 0.9 convert.14
  17.0 0.9 convert.15
  17.9 0.7 pad_maximum_fusion
  18.7 0.7 convert_bitcast_fusion
  19.4 22.2 %all-gather = bf16[16,64,13]{1,2,0:T(8,128)(2,1)S(1)} all-gather(bf16[1,64,13]{1,2,0:T(8,128)(2,1)S(1)} %convert_bitcast_fusion), channel_id=1, replica_groups=mesh['dp'=16,'tensor'=2] {'dp'}, dimensions={0}, use_global_device_ids=true | all-gather | bytes 28288 | tf_op jit(solution)/shard_map/all_gather | solution.py:313
  43.4 0.8 copy-done.14
  45.1 5.6 fusion.22
  50.7 10.2 %collective-permute-done = bf16[1024,1024]{1,0:T(8,128)(2,1)} collective-permute-done((bf16[1024,1024]{1,0:T(8,128)(2,1)}, bf16[1024,1024]{1,0:T(8,128)(2,1)}, u32[]{:S(2)}, u32[]{:S(2)}) %collective-permute-start) | collective-permute-done | bytes 2097184 | tf_op jit(solution)/shard_map/ppermute | solution.py:300
  60.9 1.9 constant_dynamic-update-slice_fusion.7
  62.9 42.2 %collective-permute-done.1 = bf16[1024,1024]{1,0:T(8,128)(2,1)} collective-permute-done((bf16[1024,1024]{1,0:T(8,128)(2,1)}, bf16[1024,1024]{1,0:T(8,128)(2,1)}, u32[]{:S(2)}, u32[]{:S(2)}) %collective-permute-start.1) | collective-permute-done | bytes 2097184 | tf_op jit(solution)/shard_map/ppermute | solution.py:300
  105.0 1.9 constant_dynamic-update-slice_fusion.5.dy_ref
  106.9 2.1 copy-done.2
  109.0 0.6 convert_reduce_fusion.1
  109.6 1.4 fusion.17
  111.0 3.0 fusion.11.normed_ref
  114.1 2.1 all-gather.9.cloned.1.call-done.out_ref
  116.2 2.2 copy-done.1
  118.4 2.2 copy-done.3
  120.6 2.2 copy-done.7
  122.8 23.1 %hidden_units.1 = (bf16[2048,2048]{1,0:T(8,128)(2,1)}, bf16[2048,2048]{1,0:T(8,128)(2,1)}) custom-call(bf16[2048,1024]{1,0:T(8,128)(2,1)S(1)} %copy-done.1, bf16[2048,1024]{1,0:T(8,128)(2,1)S(1)} %copy-done.3, bf16[1024,2048]{1,0:T(8,128)(2,1)S(1)} %copy-done.7, bf16[1024,2048]{1,0:T(8,128)(2,1)} %all-gather.9.cloned.1.call-done.out_ref, f32[1,2048]{1,0:T(1,128)S(1)} %bitcast.48), custom_call_target="tpu_custom_call" | custom-call | flops 17179869184 | bytes 41943040 | tf_op jit(solution)/shard_map/hidden_units/pallas_call | solution.py:232
  145.9 12.8 %convolution_convert_fusion.2 = bf16[1024,2048]{1,0:T(8,128)(2,1)} fusion(bf16[2048,1024]{1,0:T(8,128)(2,1)S(1)} %copy-done.1, bf16[2048,2048]{1,0:T(8,128)(2,1)} %get-tuple-element.31), kind=kOutput, calls=%fused_computation.34 | convolution fusion | flops 8592031744 | bytes 16777216 | tf_op jit(solution)/shard_map/dot_general | solution.py:59
  158.7 14.6 %convolution_convert_fusion.1 = bf16[1024,2048]{1,0:T(8,128)(2,1)} fusion(bf16[2048,1024]{1,0:T(8,128)(2,1)} %copy-done.2, bf16[2048,2048]{1,0:T(8,128)(2,1)} %get-tuple-element.32), kind=kOutput, calls=%fused_computation.33 | convolution fusion | flops 8592031744 | bytes 16777216 | tf_op jit(solution)/shard_map/dot_general | solution.py:59
  173.3 6.3 convolution_convert_fusion.3.do_ref
  179.6 9.9 %convolution_add_fusion.q_ref.k_ref.v_ref = f32[2048,1536]{1,0:T(8,128)} fusion(f32[1536]{0:T(1024)S(1)} %add.247, bf16[1024,2048]{1,0:T(8,128)(2,1)S(1)} %copy-done.38, bf16[2048,1024]{1,0:T(8,128)(2,1)S(1)} %copy-done.12, f32[1024]{0:T(1024)S(1)} %bitcast.63, f32[1024]{0:T(1024)S(1)} %bitcast.65, f32[2048]{0:T(1024)S(1)} %add_rsqrt_fusion, ...), kind=kOutput, calls=%fused_computation.11 | convolution fusion | flops 6458179584 | bytes 19955712 | tf_op jit(solution)/shard_map/dot_general | solution.py:47
  189.4 128.2 %attention.1 = (bf16[2048,512]{1,0:T(8,128)(2,1)S(1)}, bf16[2048,512]{1,0:T(8,128)(2,1)S(1)}, bf16[2048,512]{1,0:T(8,128)(2,1)S(1)}, bf16[2048,512]{1,0:T(8,128)(2,1)}) custom-call(s32[1,2048]{1,0:T(1,128)S(1)} %compare_select_fusion.first_ref, f32[2048,1536]{1,0:T(8,128)} %convolution_add_fusion.q_ref.k_ref.v_ref, ...), custom_call_target="tpu_custom_call" | custom-call | flops 60000002048 | bytes 31457280 | tf_op jit(solution)/shard_map/attention/pallas_call | solution.py:192
  317.9 1.0 copy-done
  319.0 1.8 copy-done.16
  320.9 2.7 copy-done.23
  323.6 9.2 %fusion.19 = f32[2048,1024]{1,0:T(8,128)} fusion(bf16[2048,1536]{1,0:T(8,128)(2,1)S(1)} %constant_dynamic-update-slice_fusion, bf16[1024,2048]{1,0:T(8,128)(2,1)S(1)} %copy-done.38), kind=kOutput, calls=%fused_computation.37 | convolution fusion | flops 6442450944 | bytes 17825792 | tf_op jit(solution)/shard_map/dot_general | solution.py:53
  332.7 17.8 %fusion.49 = (f32[1024]{0:T(1024)S(1)}, f32[1024]{0:T(1024)S(1)}, f32[2048]{0:T(1024)S(1)}, f32[2048]{0:T(1024)S(1)}, f32[2048,1024]{1,0:T(8,128)}, /*index=5*/f32[1024]{0:T(1024)S(1)}, f32[1024]{0:T(1024)S(1)}) fusion(f32[2048]{0:T(1024)S(1)} %add_rsqrt_fusion, f32[2048]{0:T(1024)S(1)} %broadcast_multiply_fusion.2, bf16[2048,1024]{1,0:T(8,128)(2,1)} %copy-done.11, ...), kind=kOutput, calls=%fused_computation.126 | convolution fusion | flops 8621383680 | bytes 33611776 | tf_op jit(solution)/shard_map/dot_general | solution.py:53
  350.5 6.1 fusion.14
  356.7 3.3 copy-done.13
  360.0 1.6 dynamic-slice_convert_fusion
  361.7 1.5 collective-permute-start.3
  363.1 3.4 convolution_convert_fusion.4
  366.8 4.7 convert_reduce_fusion
  371.9 2.1 convert_reduce_fusion.5
  374.8 35.0 %collective-permute-done.3 = bf16[1024,1024]{1,0:T(8,128)(2,1)} collective-permute-done((bf16[1024,1024]{1,0:T(8,128)(2,1)}, bf16[1024,1024]{1,0:T(8,128)(2,1)}, u32[]{:S(2)}, u32[]{:S(2)}) %collective-permute-start.3) | collective-permute-done | bytes 2097184 | tf_op jit(solution)/shard_map/ppermute | solution.py:310
  409.8 5.5 convert_reduce_fusion.2
  415.4 1.0 copy.52
  416.5 11.9 %convolution_convert_fusion = bf16[1024,1536]{1,0:T(8,128)(2,1)} fusion(bf16[2048,1536]{1,0:T(8,128)(2,1)} %copy-done.23, bf16[2048,1024]{1,0:T(8,128)(2,1)} %copy-done.11, f32[1024]{0:T(1024)S(1)} %bitcast.64, f32[1024]{0:T(1024)S(1)} %bitcast.67, f32[2048]{0:T(1024)S(1)} %add_rsqrt_fusion, f32[2048]{0:T(1024)S(1)} %broadcast_multiply_fusion.2), kind=kOutput, calls=%fused_computation.32 | convolution fusion | flops 6456606720 | bytes 13656064 | tf_op jit(solution)/shard_map/dot_general | solution.py:59
  428.5 0.7 reduce-scatter.12.cloned.1.call-update
  430.0 7.1 fusion.26
  437.1 12.7 %convolution_add_fusion.1 = f32[2048,1024]{1,0:T(8,128)S(1)} fusion(f32[2048,1024]{1,0:T(8,128)} %fusion.26, bf16[2048,2048]{1,0:T(8,128)(2,1)} %get-tuple-element.32, bf16[1024,2048]{1,0:T(8,128)(2,1)S(1)} %copy-done.37), kind=kOutput, calls=%fused_computation.35 | convolution fusion | flops 8592031744 | bytes 29360128 | tf_op jit(solution)/shard_map/dot_general | solution.py:53
  449.8 3.2 copy-done.20
  453.0 1.6 dynamic-slice_convert_fusion.1
  454.7 1.5 collective-permute-start.2
  456.2 1.6 multiply_subtract_fusion.2
  457.8 44.2 %collective-permute-done.2 = bf16[1024,1024]{1,0:T(8,128)(2,1)} collective-permute-done((bf16[1024,1024]{1,0:T(8,128)(2,1)}, bf16[1024,1024]{1,0:T(8,128)(2,1)}, u32[]{:S(2)}, u32[]{:S(2)}) %collective-permute-start.2) | collective-permute-done | bytes 2097184 | tf_op jit(solution)/shard_map/ppermute | solution.py:310
  502.1 5.7 add_convert_fusion
  507.8 0.9 copy.53
  508.7 5.0 psum.7
  513.7 1.3 multiply_subtract_fusion.6
  515.1 36.5 %reduce-scatter.8.cloned.1.call-done = bf16[64,1536]{1,0:T(8,128)(2,1)} async-done(((bf16[1024,1536]{1,0:T(8,128)(2,1)}), bf16[64,1536]{1,0:T(8,128)(2,1)}) %reduce-scatter.8.cloned.1.call-update) | async-done | bytes 196624 | tf_op jit(solution)/shard_map/reduce_scatter | solution.py:347
  551.6 2.4 multiply_subtract_fusion.3
  553.9 72.8 %reduce-scatter.12.cloned.1.call-done = bf16[64,2048]{1,0:T(8,128)(2,1)} async-done(((bf16[1024,2048]{1,0:T(8,128)(2,1)}), bf16[64,2048]{1,0:T(8,128)(2,1)}) %reduce-scatter.12.cloned.1.call-update) | async-done | bytes 262160 | tf_op jit(solution)/shard_map/reduce_scatter | solution.py:347
  626.7 2.5 multiply_subtract_fusion.1
  629.2 73.6 %reduce-scatter.14.cloned.1.call-done = bf16[64,2048]{1,0:T(8,128)(2,1)} async-done(((bf16[1024,2048]{1,0:T(8,128)(2,1)}), bf16[64,2048]{1,0:T(8,128)(2,1)}) %reduce-scatter.14.cloned.1.call-update) | async-done | bytes 262160 | tf_op jit(solution)/shard_map/reduce_scatter | solution.py:347
  702.8 2.3 multiply_subtract_fusion
  (129 shorter events, 5.8 us)
Async XLA Ops:
  7.2 35.4 %copy-start.18 = (bf16[1024,1024]{1,0:T(8,128)(2,1)S(1)}, bf16[1024,1024]{1,0:T(8,128)(2,1)}, u32[]{:S(2)}) copy-start(bf16[1024,1024]{1,0:T(8,128)(2,1)} %param.25) | copy-start | bytes 6291460
  7.2 34.6 %copy-start.36 = (s32[1,2]{1,0:T(1,128)S(1)}, s32[1,2]{1,0:T(1,128)}, u32[]{:S(2)}) copy-start(s32[1,2]{1,0:T(1,128)} %param.28) | copy-start | bytes 28
  7.2 34.6 %copy-start.39 = (s32[1,2]{1,0:T(1,128)S(1)}, s32[1,2]{1,0:T(1,128)}, u32[]{:S(2)}) copy-start(s32[1,2]{1,0:T(1,128)} %param.27) | copy-start | bytes 28
  7.2 106.8 %all-gather.7.cloned.1.call-start = ((), (), s32[]{:S(2)}) async-start(), calls=%async_computation.6 | async-start | bytes 4456448 | tf_op jit(solution)/shard_map/all_gather | solution.py:313
  9.2 107.0 %all-gather.9.cloned.1.call-start = ((), (), s32[]{:S(2)}) async-start(), calls=%async_computation.7 | async-start | bytes 4456448 | tf_op jit(solution)/shard_map/all_gather | solution.py:313
  11.1 162.2 %all-gather.5.cloned.1.call-start = ((), (), s32[]{:S(2)}) async-start(), calls=%async_computation.5 | async-start | bytes 4456448 | tf_op jit(solution)/shard_map/all_gather | solution.py:313
  11.1 49.8 %collective-permute-start = (bf16[1024,1024]{1,0:T(8,128)(2,1)}, bf16[1024,1024]{1,0:T(8,128)(2,1)}, u32[]{:S(2)}, u32[]{:S(2)}) collective-permute-start(bf16[1024,1024]{1,0:T(8,128)(2,1)} %param.25), channel_id=1, source_target_pairs={{0,1},{1,0},{2,3},{3,2},{4,5},{5,4},{6,7},{7,6},{8,9},{9,8},{10,11... | collective-permute-start | bytes 6291464 | tf_op jit(solution)/shard_map/ppermute | solution.py:300
  14.1 90.9 %collective-permute-start.1 = (bf16[1024,1024]{1,0:T(8,128)(2,1)}, bf16[1024,1024]{1,0:T(8,128)(2,1)}, u32[]{:S(2)}, u32[]{:S(2)}) collective-permute-start(bf16[1024,1024]{1,0:T(8,128)(2,1)} %param.26), channel_id=1, source_target_pairs={{0,1},{1,0},{2,3},{3,2},{4,5},{5,4},{6,7},{7,6},{8,9},{9,8},{10,11... | collective-permute-start | bytes 6291464 | tf_op jit(solution)/shard_map/ppermute | solution.py:300
  18.6 437.5 %reduce-scatter.10.cloned.1.call-start = ((), (), s32[]{:S(2)}) async-start(), calls=%async_computation.9 | async-start | bytes 1114112 | tf_op jit(solution)/shard_map/reduce_scatter | solution.py:347
  42.6 1.6 copy-start.14
  62.8 48.2 %copy-start.11 = (bf16[2048,1024]{1,0:T(8,128)(2,1)}, bf16[2048,1024]{1,0:T(8,128)(2,1)S(1)}, u32[]{:S(2)}) copy-start(bf16[2048,1024]{1,0:T(8,128)(2,1)S(1)} %constant_dynamic-update-slice_fusion.7) | copy-start | bytes 12582916
  106.9 2.1 copy-start.2
  116.2 2.2 copy-start.1
  118.4 2.2 copy-start.3
  120.6 2.2 copy-start.7
  173.3 6.3 copy-start.12
  173.3 6.3 copy-start.38
  179.6 9.9 %copy-start.5 = (f32[2048,128]{1,0:T(8,128)S(1)}, f32[2048,128]{1,0:T(8,128)}, u32[]{:S(2)}) copy-start(f32[2048,128]{1,0:T(8,128)} %get-tuple-element.92.qahead_ref.ahead_ref) | copy-start | bytes 3145732
  179.6 9.9 %copy-start.6 = (f32[2048,128]{1,0:T(8,128)S(1)}, f32[2048,128]{1,0:T(8,128)}, u32[]{:S(2)}) copy-start(f32[2048,128]{1,0:T(8,128)} %get-tuple-element.93.qkeep_ref.keep_ref) | copy-start | bytes 3145732
  317.6 1.3 copy-start
  317.6 45.5 %copy-start.9 = (bf16[2048,512]{1,0:T(8,128)(2,1)}, bf16[2048,512]{1,0:T(8,128)(2,1)S(1)}, u32[]{:S(2)}) copy-start(bf16[2048,512]{1,0:T(8,128)(2,1)S(1)} %get-tuple-element.35) | copy-start | bytes 6291460
  317.7 3.1 copy-start.16
  320.9 2.7 copy-start.23
  323.6 9.2 %copy-start.8 = (bf16[1024,2048]{1,0:T(8,128)(2,1)S(1)}, bf16[1024,2048]{1,0:T(8,128)(2,1)}, u32[]{:S(2)}) copy-start(bf16[1024,2048]{1,0:T(8,128)(2,1)} %all-gather.7.cloned.1.call-done.in_ref) | copy-start | bytes 12582916
  356.7 3.4 copy-start.13
  360.0 3.1 copy-start.4
  361.7 48.1 %collective-permute-start.3 = (bf16[1024,1024]{1,0:T(8,128)(2,1)}, bf16[1024,1024]{1,0:T(8,128)(2,1)}, u32[]{:S(2)}, u32[]{:S(2)}) collective-permute-start(bf16[1024,1024]{1,0:T(8,128)(2,1)} %dynamic-slice_convert_fusion), channel_id=1, source_target_pairs={{0,1},{1,0},{2,3},{3,2},{4,5},{5,4},{6,7},{7,6},{8,9},{9,8},{10,11... | collective-permute-start | bytes 6291464 | tf_op jit(solution)/shard_map/ppermute | solution.py:310
  366.6 141.2 %reduce-scatter.16.cloned.1.call-start = ((), (), s32[]{:S(2)}) async-start(), calls=%async_computation.12 | async-start | bytes 557056
  371.9 2.5 copy-start.17
  371.9 37.9 %copy-start.15 = (bf16[1024,1024]{1,0:T(8,128)(2,1)S(1)}, bf16[1024,1024]{1,0:T(8,128)(2,1)}, u32[]{:S(2)}) copy-start(bf16[1024,1024]{1,0:T(8,128)(2,1)} %param.26) | copy-start | bytes 6291460
  416.4 135.1 %reduce-scatter.8.cloned.1.call-start = ((), (), s32[]{:S(2)}) async-start(), calls=%async_computation.8 | async-start | bytes 3342336 | tf_op jit(solution)/shard_map/reduce_scatter | solution.py:347
  428.4 1.6 copy-start.10
  428.4 198.3 %reduce-scatter.12.cloned.1.call-start = ((), (), s32[]{:S(2)}) async-start(), calls=%async_computation.10 | async-start | bytes 4456448 | tf_op jit(solution)/shard_map/reduce_scatter | solution.py:347
  429.2 273.7 %reduce-scatter.14.cloned.1.call-start = ((), (), s32[]{:S(2)}) async-start(), calls=%async_computation.11 | async-start | bytes 4456448 | tf_op jit(solution)/shard_map/reduce_scatter | solution.py:347
  430.0 7.1 copy-start.37
  449.8 3.2 copy-start.20
  453.0 3.2 copy-start.27
  453.0 3.2 copy-start.31
  453.0 3.2 copy-start.32
  453.0 49.0 %copy-start.19 = (bf16[1024,1024]{1,0:T(8,128)(2,1)S(1)}, bf16[1024,1024]{1,0:T(8,128)(2,1)}, u32[]{:S(2)}) copy-start(bf16[1024,1024]{1,0:T(8,128)(2,1)} %param.25) | copy-start | bytes 6291460
  453.0 49.0 %copy-start.34 = (f32[1024,1]{0,1:T(1,128)S(1)}, f32[1024,1]{0,1:T(1,128)}, u32[]{:S(2)}) copy-start(f32[1024,1]{0,1:T(1,128)} %get-tuple-element.85) | copy-start | bytes 12292
  453.0 49.0 %copy-start.35 = (f32[1024,1]{0,1:T(1,128)S(1)}, f32[1024,1]{0,1:T(1,128)}, u32[]{:S(2)}) copy-start(f32[1024,1]{0,1:T(1,128)} %get-tuple-element.86) | copy-start | bytes 12292
  454.7 47.3 %collective-permute-start.2 = (bf16[1024,1024]{1,0:T(8,128)(2,1)}, bf16[1024,1024]{1,0:T(8,128)(2,1)}, u32[]{:S(2)}, u32[]{:S(2)}) collective-permute-start(bf16[1024,1024]{1,0:T(8,128)(2,1)} %dynamic-slice_convert_fusion.1), channel_id=1, source_target_pairs={{0,1},{1,0},{2,3},{3,2},{4,5},{5,4},{6,7},{7,6},{8,9},{9,8},{10,11... | collective-permute-start | bytes 6291464 | tf_op jit(solution)/shard_map/ppermute | solution.py:310
  502.0 11.7 %copy-start.33 = (f32[64,13]{0,1:T(8,128)S(1)}, f32[64,13]{0,1:T(8,128)}, u32[]{:S(2)}) copy-start(f32[64,13]{0,1:T(8,128)} %param.35) | copy-start | bytes 9988
  502.0 49.5 %copy-start.24 = (f32[64,512]{1,0:T(8,128)S(1)}, f32[64,512]{1,0:T(8,128)}, u32[]{:S(2)}) copy-start(f32[64,512]{1,0:T(8,128)} %param.31) | copy-start | bytes 393220
  502.0 49.5 %copy-start.25 = (f32[64,512]{1,0:T(8,128)S(1)}, f32[64,512]{1,0:T(8,128)}, u32[]{:S(2)}) copy-start(f32[64,512]{1,0:T(8,128)} %param.30) | copy-start | bytes 393220
  502.1 49.5 %copy-start.26 = (f32[64,512]{1,0:T(8,128)S(1)}, f32[64,512]{1,0:T(8,128)}, u32[]{:S(2)}) copy-start(f32[64,512]{1,0:T(8,128)} %param.29) | copy-start | bytes 393220
  502.1 124.6 %copy-start.21 = (f32[64,2048]{1,0:T(8,128)S(1)}, f32[64,2048]{1,0:T(8,128)}, u32[]{:S(2)}) copy-start(f32[64,2048]{1,0:T(8,128)} %param.33) | copy-start | bytes 1572868
  502.1 124.6 %copy-start.28 = (f32[64,2048]{1,0:T(8,128)S(1)}, f32[64,2048]{1,0:T(8,128)}, u32[]{:S(2)}) copy-start(f32[64,2048]{1,0:T(8,128)} %param.47) | copy-start | bytes 1572868
  507.8 195.1 %copy-start.22 = (f32[64,2048]{1,0:T(8,128)S(1)}, f32[64,2048]{1,0:T(8,128)}, u32[]{:S(2)}) copy-start(f32[64,2048]{1,0:T(8,128)} %param.34) | copy-start | bytes 1572868
  507.8 195.1 %copy-start.29 = (f32[64,2048]{1,0:T(8,128)S(1)}, f32[64,2048]{1,0:T(8,128)}, u32[]{:S(2)}) copy-start(f32[64,2048]{1,0:T(8,128)} %param.48) | copy-start | bytes 1572868
  507.8 195.1 %copy-start.30 = (f32[64,2048]{1,0:T(8,128)S(1)}, f32[64,2048]{1,0:T(8,128)}, u32[]{:S(2)}) copy-start(f32[64,2048]{1,0:T(8,128)} %param.41) | copy-start | bytes 1572868
Sparse Core Ops, SparseCore 0:
  10.8 53.5 all-gather.6
  67.1 49.0 all-gather.8
  118.9 49.2 all-gather.4
  366.7 56.6 reduce-scatter.9
  427.8 54.7 reduce-scatter.15
  486.2 65.2 reduce-scatter.7
  555.4 71.2 reduce-scatter.11
  631.1 71.7 reduce-scatter.13

commit v2 on v1

--- a/solution.py
+++ b/solution.py
@@ -358,6 +358,11 @@
     attended, grad_query_lin, grad_key_lin, grad_value_lin = attention(
         first_row, lin, grad_attended, rotary_tables(position)
     )
+    attended, grad_query_lin, grad_key_lin, grad_value_lin, sum_in, sum_out = (
+        lax.optimization_barrier(
+            (attended, grad_query_lin, grad_key_lin, grad_value_lin, sum_in, sum_out)
+        )
+    )
     grad_qkv_lin = jnp.concatenate([grad_query_lin, grad_key_lin, grad_value_lin], axis=1)
     grad_qkv = dot_tn(normed_one, grad_qkv_lin).astype(low)
     sum_qkv = spread(grad_qkv)

time: 721 us -> 584 us (0.81)
  waiting for transfers between devices: 318 us -> 175 us
  starting transfers between devices: 6.86 us -> 17.6 us
    reduce_scatter x4, waiting for transfers between devices: 183 us -> 37.9 us  [spread(): return lax.psum_scatter(values, 'dp', scatter_dimension=0, tiled=True)]
    reduce_scatter x4, starting transfers between devices: 0.42 us -> 11.4 us  [spread(): return lax.psum_scatter(values, 'dp', scatter_dimension=0, tiled=True)]
    unnamed x86 -> x110, local copies, waits for them, and re-layouts: 23.9 us -> 26.5 us
  transfers between devices with their start and end apart: 12 -> 12, of which waited for: 8 -> 6; matrix products, arithmetic and copies ran while one was open for 16% -> 23% of each run, Pallas kernels for 3% -> 26%
where the time goes in v2:
time: 584 us; the launch traced here: 581 us
  waiting for transfers between devices  175 us (30%)
  Pallas kernels  151 us (26%)
  matrix products  107 us (18%)
  other arithmetic  51.9 us (9%)
  local copies, waits for them, and re-layouts  36.5 us (6%)
  blocking collectives  27.2 us (5%)
  starting transfers between devices  17.6 us (3%)
  between operations  15 us (3%)
    pallas_call x1, Pallas kernels, attention(): pl.pallas_call(attention_kernel, grid=(pairs, blocks), in_specs=[pl.Block...  127 us
    ppermute x2, waiting for transfers between devices, summed_rows(): lax.ppermute(theirs.astype(low), 'tensor', swap).astype(jnp.float32)  76.6 us
    ppermute x2, waiting for transfers between devices, both_rows(): other = lax.ppermute(mine, 'tensor', swap)  58.3 us
    dot_general x4, matrix products, dot_nt(): lax.dot_general(left, right, (((1,), (1,)), ((), ())), preferred_element_...  46.8 us
    dot_general x4, matrix products, dot_tn(): lax.dot_general(left, right, (((0,), (0,)), ((), ())), preferred_element_...  42.9 us
    reduce_scatter x4, waiting for transfers between devices, spread(): return lax.psum_scatter(values, 'dp', scatter_dimension=0, tiled=True)  37.9 us
    unnamed x110, local copies, waits for them, and re-layouts  26.5 us
    pallas_call x1, Pallas kernels, hidden_units(): pl.pallas_call(hidden_kernel, grid=(units // tile_units, rows // tile_row...  23.1 us
  transfers between devices with their start and end apart: 12, of which 6 were waited for; matrix products, arithmetic and copies ran while one was open for 23% of the time, Pallas kernels for 26%

profile of v2, /device:TPU:0, one launch (start us, length us, event | category | flops | bytes accessed | tf_op | source)
XLA Modules:
  0.0 581.0 jit_solution(7294215994099014748)
XLA Ops:
  7.2 1.9 convert_element_type.117
  9.2 1.8 convert_element_type.118
  11.1 3.0 collective-permute-start
  14.1 0.9 convert.12
  15.0 0.9 convert.13
  16.0 0.9 convert.14
  16.9 0.9 convert.15
  17.8 0.7 pad_maximum_fusion
  18.7 0.7 convert_bitcast_fusion
  19.4 22.2 %all-gather = bf16[16,64,13]{1,2,0:T(8,128)(2,1)S(1)} all-gather(bf16[1,64,13]{1,2,0:T(8,128)(2,1)S(1)} %convert_bitcast_fusion), channel_id=1, replica_groups=mesh['dp'=16,'tensor'=2] {'dp'}, dimensions={0}, use_global_device_ids=true | all-gather | bytes 28288 | tf_op jit(solution)/shard_map/all_gather | solution.py:313
  43.2 0.8 copy-done.15
  44.2 0.6 fusion.65
  44.8 16.1 %collective-permute-done = bf16[1024,1024]{1,0:T(8,128)(2,1)} collective-permute-done((bf16[1024,1024]{1,0:T(8,128)(2,1)}, bf16[1024,1024]{1,0:T(8,128)(2,1)}, u32[]{:S(2)}, u32[]{:S(2)}) %collective-permute-start) | collective-permute-done | bytes 2097184 | tf_op jit(solution)/shard_map/ppermute | solution.py:300
  60.9 1.9 constant_dynamic-update-slice_fusion.7
  62.8 42.2 %collective-permute-done.1 = bf16[1024,1024]{1,0:T(8,128)(2,1)} collective-permute-done((bf16[1024,1024]{1,0:T(8,128)(2,1)}, bf16[1024,1024]{1,0:T(8,128)(2,1)}, u32[]{:S(2)}, u32[]{:S(2)}) %collective-permute-start.1) | collective-permute-done | bytes 2097184 | tf_op jit(solution)/shard_map/ppermute | solution.py:300
  105.0 1.9 constant_dynamic-update-slice_fusion.5.dy_ref
  106.9 2.1 copy-done.2
  108.9 0.6 convert_reduce_fusion.1
  109.6 1.4 fusion.17
  111.0 3.1 fusion.11.normed_ref
  114.1 2.1 all-gather.9.cloned.1.call-done.out_ref
  116.2 2.2 copy-done.1
  118.4 2.2 copy-done.3
  120.5 2.2 copy-done.8
  122.7 23.1 %hidden_units.1 = (bf16[2048,2048]{1,0:T(8,128)(2,1)}, bf16[2048,2048]{1,0:T(8,128)(2,1)}) custom-call(bf16[2048,1024]{1,0:T(8,128)(2,1)S(1)} %copy-done.1, bf16[2048,1024]{1,0:T(8,128)(2,1)S(1)} %copy-done.3, bf16[1024,2048]{1,0:T(8,128)(2,1)S(1)} %copy-done.8, bf16[1024,2048]{1,0:T(8,128)(2,1)} %all-gather.9.cloned.1.call-done.out_ref, f32[1,2048]{1,0:T(1,128)S(1)} %bitcast.48), custom_call_target="tpu_custom_call" | custom-call | flops 17179869184 | bytes 41943040 | tf_op jit(solution)/shard_map/hidden_units/pallas_call | solution.py:232
  145.8 12.8 %convolution_convert_fusion.2 = bf16[1024,2048]{1,0:T(8,128)(2,1)} fusion(bf16[2048,1024]{1,0:T(8,128)(2,1)S(1)} %copy-done.1, bf16[2048,2048]{1,0:T(8,128)(2,1)} %get-tuple-element.37), kind=kOutput, calls=%fused_computation.34 | convolution fusion | flops 8592031744 | bytes 16777216 | tf_op jit(solution)/shard_map/dot_general | solution.py:59
  158.7 11.2 %reduce-scatter.10.cloned.1.call-start = ((), (), s32[]{:S(2)}) async-start(), calls=%async_computation.9 | async-start | bytes 4456448 | tf_op jit(solution)/shard_map/reduce_scatter | solution.py:347
  170.2 5.6 fusion.22
  175.8 14.4 %convolution_convert_fusion.1 = bf16[1024,2048]{1,0:T(8,128)(2,1)} fusion(bf16[2048,1024]{1,0:T(8,128)(2,1)} %copy-done.2, bf16[2048,2048]{1,0:T(8,128)(2,1)} %get-tuple-element.38), kind=kOutput, calls=%fused_computation.33 | convolution fusion | flops 8592031744 | bytes 16777216 | tf_op jit(solution)/shard_map/dot_general | solution.py:59
  190.4 12.5 %convolution_add_fusion.q_ref.k_ref.v_ref = f32[2048,1536]{1,0:T(8,128)} fusion(f32[1536]{0:T(1024)S(1)} %add.247, bf16[1024,2048]{1,0:T(8,128)(2,1)} %all-gather.5.cloned.1.call-done, bf16[2048,1024]{1,0:T(8,128)(2,1)} %copy-done.13, f32[1024]{0:T(1024)S(1)} %bitcast.63, f32[1024]{0:T(1024)S(1)} %bitcast.65, f32[2048]{0:T(1024)S(1)} %add_rsqrt_fusion, ...), kind=kOutput, calls=%fused_computation.11 | convolution fusion | flops 6458179584 | bytes 19953664 | tf_op jit(solution)/shard_map/dot_general | solution.py:47
  202.9 5.1 convolution_convert_fusion.3.do_ref
  208.0 127.5 %attention.1 = (bf16[2048,512]{1,0:T(8,128)(2,1)S(1)}, bf16[2048,512]{1,0:T(8,128)(2,1)S(1)}, bf16[2048,512]{1,0:T(8,128)(2,1)S(1)}, bf16[2048,512]{1,0:T(8,128)(2,1)}) custom-call(s32[1,2048]{1,0:T(1,128)S(1)} %compare_select_fusion.first_ref, f32[2048,1536]{1,0:T(8,128)} %convolution_add_fusion.q_ref.k_ref.v_ref, ...), custom_call_target="tpu_custom_call" | custom-call | flops 60000002048 | bytes 31457280 | tf_op jit(solution)/shard_map/attention/pallas_call | solution.py:192
  335.5 1.3 copy-done
  336.8 1.3 copy-done.10
  338.1 1.9 constant_dynamic-update-slice_fusion.2
  340.5 3.0 copy-done.24
  344.0 8.9 %fusion.19 = f32[2048,1024]{1,0:T(8,128)} fusion(bf16[2048,1536]{1,0:T(8,128)(2,1)S(1)} %constant_dynamic-update-slice_fusion, bf16[1024,2048]{1,0:T(8,128)(2,1)S(1)} %copy-done.50), kind=kOutput, calls=%fused_computation.37 | convolution fusion | flops 6442450944 | bytes 17825792 | tf_op jit(solution)/shard_map/dot_general | solution.py:53
  353.0 18.1 %fusion.49 = (f32[1024]{0:T(1024)S(1)}, f32[1024]{0:T(1024)S(1)}, f32[2048]{0:T(1024)S(1)}, f32[2048]{0:T(1024)S(1)}, f32[2048,1024]{1,0:T(8,128)}, /*index=5*/f32[1024]{0:T(1024)S(1)}, f32[1024]{0:T(1024)S(1)}) fusion(f32[2048]{0:T(1024)S(1)} %add_rsqrt_fusion, f32[2048]{0:T(1024)S(1)} %broadcast_multiply_fusion.2, bf16[2048,1024]{1,0:T(8,128)(2,1)} %copy-done.13, ...), kind=kOutput, calls=%fused_computation.126 | convolution fusion | flops 8621383680 | bytes 33611776 | tf_op jit(solution)/shard_map/dot_general | solution.py:53
  371.1 6.3 %fusion.14 = f32[2048,1024]{1,0:T(8,128)S(1)} fusion(bf16[2048,1024]{1,0:T(8,128)(2,1)} %copy-done.13, f32[2048,1024]{1,0:T(8,128)} %get-tuple-element.86, f32[2048]{0:T(1024)S(1)} %broadcast_multiply_fusion, f32[2048]{0:T(1024)S(1)} %broadcast_multiply_fusion.1, f32[2048]{0:T(1024)S(1)} %add_rsqrt_fusion, f32[2048]{0:T(1024)S(1)} %broadcast_multiply_fusion.2), kind=kLoop, calls=%fused_computation.18 | loop fusion | flops 14680064 | bytes 21004288 | tf_op jit(solution)/shard_map/mul | solution.py:375
  377.4 3.3 copy-done.14
  380.7 1.7 dynamic-slice_convert_fusion
  382.3 1.5 collective-permute-start.3
  383.8 3.4 convolution_convert_fusion.4
  387.3 4.7 convert_reduce_fusion
  392.4 2.1 convert_reduce_fusion.5
  395.2 35.2 %collective-permute-done.3 = bf16[1024,1024]{1,0:T(8,128)(2,1)} collective-permute-done((bf16[1024,1024]{1,0:T(8,128)(2,1)}, bf16[1024,1024]{1,0:T(8,128)(2,1)}, u32[]{:S(2)}, u32[]{:S(2)}) %collective-permute-start.3) | collective-permute-done | bytes 2097184 | tf_op jit(solution)/shard_map/ppermute | solution.py:310
  430.5 5.5 convert_reduce_fusion.2
  436.1 1.0 copy.52
  437.2 12.3 %convolution_convert_fusion = bf16[1024,1536]{1,0:T(8,128)(2,1)} fusion(bf16[2048,1536]{1,0:T(8,128)(2,1)} %copy-done.24, bf16[2048,1024]{1,0:T(8,128)(2,1)} %copy-done.13, f32[1024]{0:T(1024)S(1)} %bitcast.64, f32[1024]{0:T(1024)S(1)} %bitcast.67, f32[2048]{0:T(1024)S(1)} %add_rsqrt_fusion, f32[2048]{0:T(1024)S(1)} %broadcast_multiply_fusion.2), kind=kOutput, calls=%fused_computation.32 | convolution fusion | flops 6456606720 | bytes 13656064 | tf_op jit(solution)/shard_map/dot_general | solution.py:59
  449.5 7.0 %fusion.26 = f32[2048,1024]{1,0:T(8,128)} fusion(bf16[2048,512]{1,0:T(8,128)(2,1)S(1)} %copy-done.12, bf16[1024,2048]{1,0:T(8,128)(2,1)} %all-gather.5.cloned.1.call-done), kind=kOutput, calls=%fused_computation.47 | convolution fusion | flops 2147483648 | bytes 11534336 | tf_op jit(solution)/shard_map/dot_general | solution.py:53
  456.5 12.7 %convolution_add_fusion.1 = f32[2048,1024]{1,0:T(8,128)S(1)} fusion(f32[2048,1024]{1,0:T(8,128)} %fusion.26, bf16[2048,2048]{1,0:T(8,128)(2,1)} %get-tuple-element.38, bf16[1024,2048]{1,0:T(8,128)(2,1)S(1)} %copy-done.49), kind=kOutput, calls=%fused_computation.35 | convolution fusion | flops 8592031744 | bytes 29360128 | tf_op jit(solution)/shard_map/dot_general | solution.py:53
  469.2 3.3 copy-done.21
  472.6 1.7 dynamic-slice_convert_fusion.1
  474.3 1.5 collective-permute-start.2
  475.8 1.4 multiply_subtract_fusion.1
  477.2 1.4 multiply_subtract_fusion
  478.6 1.6 multiply_subtract_fusion.2
  480.3 41.4 %collective-permute-done.2 = bf16[1024,1024]{1,0:T(8,128)(2,1)} collective-permute-done((bf16[1024,1024]{1,0:T(8,128)(2,1)}, bf16[1024,1024]{1,0:T(8,128)(2,1)}, u32[]{:S(2)}, u32[]{:S(2)}) %collective-permute-start.2) | collective-permute-done | bytes 2097184 | tf_op jit(solution)/shard_map/ppermute | solution.py:310
  521.8 5.8 add_convert_fusion
  527.6 0.8 copy.53
  528.4 5.0 psum.7
  533.4 0.6 multiply_subtract_fusion.6
  534.0 37.9 %reduce-scatter.12.cloned.1.call-done = bf16[64,1536]{1,0:T(8,128)(2,1)} async-done(((bf16[1024,1536]{1,0:T(8,128)(2,1)}), bf16[64,1536]{1,0:T(8,128)(2,1)}) %reduce-scatter.12.cloned.1.call-update) | async-done | bytes 196624 | tf_op jit(solution)/shard_map/reduce_scatter | solution.py:347
  572.0 2.0 multiply_subtract_fusion.3
  (153 shorter events, 5.0 us)
Async XLA Ops:
  7.2 35.1 %copy-start.19 = (bf16[1024,1024]{1,0:T(8,128)(2,1)S(1)}, bf16[1024,1024]{1,0:T(8,128)(2,1)}, u32[]{:S(2)}) copy-start(bf16[1024,1024]{1,0:T(8,128)(2,1)} %param.25) | copy-start | bytes 6291460
  7.2 106.9 %all-gather.7.cloned.1.call-start = ((), (), s32[]{:S(2)}) async-start(), calls=%async_computation.6 | async-start | bytes 4456448 | tf_op jit(solution)/shard_map/all_gather | solution.py:313
  9.2 107.0 %all-gather.9.cloned.1.call-start = ((), (), s32[]{:S(2)}) async-start(), calls=%async_computation.7 | async-start | bytes 4456448 | tf_op jit(solution)/shard_map/all_gather | solution.py:313
  11.0 179.3 %all-gather.5.cloned.1.call-start = ((), (), s32[]{:S(2)}) async-start(), calls=%async_computation.5 | async-start | bytes 4456448 | tf_op jit(solution)/shard_map/all_gather | solution.py:313
  11.1 49.8 %collective-permute-start = (bf16[1024,1024]{1,0:T(8,128)(2,1)}, bf16[1024,1024]{1,0:T(8,128)(2,1)}, u32[]{:S(2)}, u32[]{:S(2)}) collective-permute-start(bf16[1024,1024]{1,0:T(8,128)(2,1)} %param.25), channel_id=1, source_target_pairs={{0,1},{1,0},{2,3},{3,2},{4,5},{5,4},{6,7},{7,6},{8,9},{9,8},{10,11... | collective-permute-start | bytes 6291464 | tf_op jit(solution)/shard_map/ppermute | solution.py:300
  18.5 319.6 %reduce-scatter.8.cloned.1.call-start = ((), (), s32[]{:S(2)}) async-start(), calls=%async_computation.8 | async-start | bytes 4456448 | tf_op jit(solution)/shard_map/reduce_scatter | solution.py:347
  18.6 86.4 %collective-permute-start.1 = (bf16[1024,1024]{1,0:T(8,128)(2,1)}, bf16[1024,1024]{1,0:T(8,128)(2,1)}, u32[]{:S(2)}, u32[]{:S(2)}) collective-permute-start(bf16[1024,1024]{1,0:T(8,128)(2,1)} %param.26), channel_id=1, source_target_pairs={{0,1},{1,0},{2,3},{3,2},{4,5},{5,4},{6,7},{7,6},{8,9},{9,8},{10,11... | collective-permute-start | bytes 6291464 | tf_op jit(solution)/shard_map/ppermute | solution.py:300
  42.3 1.6 copy-start.15
  62.8 48.2 %copy-start.13 = (bf16[2048,1024]{1,0:T(8,128)(2,1)}, bf16[2048,1024]{1,0:T(8,128)(2,1)S(1)}, u32[]{:S(2)}) copy-start(bf16[2048,1024]{1,0:T(8,128)(2,1)S(1)} %constant_dynamic-update-slice_fusion.7) | copy-start | bytes 12582916
  106.9 2.1 copy-start.2
  116.2 2.2 copy-start.1
  118.4 2.2 copy-start.3
  120.5 2.2 copy-start.8
  158.6 11.4 %copy-start.48 = (s32[1,2]{1,0:T(1,128)S(1)}, s32[1,2]{1,0:T(1,128)}, u32[]{:S(2)}) copy-start(s32[1,2]{1,0:T(1,128)} %param.28) | copy-start | bytes 28
  158.6 11.4 %copy-start.51 = (s32[1,2]{1,0:T(1,128)S(1)}, s32[1,2]{1,0:T(1,128)}, u32[]{:S(2)}) copy-start(s32[1,2]{1,0:T(1,128)} %param.27) | copy-start | bytes 28
  158.7 179.4 %reduce-scatter.10.cloned.1.call-start = ((), (), s32[]{:S(2)}) async-start(), calls=%async_computation.9 | async-start | bytes 4456448 | tf_op jit(solution)/shard_map/reduce_scatter | solution.py:347
  190.3 288.3 %reduce-scatter.14.cloned.1.call-start = ((), (), s32[]{:S(2)}) async-start(), calls=%async_computation.11 | async-start | bytes 1114112 | tf_op jit(solution)/shard_map/reduce_scatter | solution.py:347
  190.4 12.5 %copy-start.4 = (bf16[2048,1024]{1,0:T(8,128)(2,1)S(1)}, bf16[2048,1024]{1,0:T(8,128)(2,1)}, u32[]{:S(2)}) copy-start(bf16[2048,1024]{1,0:T(8,128)(2,1)} %copy-done.2) | copy-start | bytes 12582916
  202.9 5.1 copy-start.6
  202.9 5.1 copy-start.7
  335.4 1.3 copy-start
  336.8 1.3 copy-start.10
  338.1 2.2 copy-start.17
  340.0 4.0 copy-start.50
  340.5 3.0 copy-start.24
  344.0 9.0 %copy-start.9 = (bf16[1024,2048]{1,0:T(8,128)(2,1)S(1)}, bf16[1024,2048]{1,0:T(8,128)(2,1)}, u32[]{:S(2)}) copy-start(bf16[1024,2048]{1,0:T(8,128)(2,1)} %all-gather.7.cloned.1.call-done.in_ref) | copy-start | bytes 12582916
  371.1 12.7 %copy-start.11 = (bf16[2048,512]{1,0:T(8,128)(2,1)S(1)}, bf16[2048,512]{1,0:T(8,128)(2,1)}, u32[]{:S(2)}) copy-start(bf16[2048,512]{1,0:T(8,128)(2,1)} %copy-done.10) | copy-start | bytes 6291460
  377.4 3.3 copy-start.14
  380.7 3.1 copy-start.5
  382.3 48.1 %collective-permute-start.3 = (bf16[1024,1024]{1,0:T(8,128)(2,1)}, bf16[1024,1024]{1,0:T(8,128)(2,1)}, u32[]{:S(2)}, u32[]{:S(2)}) collective-permute-start(bf16[1024,1024]{1,0:T(8,128)(2,1)} %dynamic-slice_convert_fusion), channel_id=1, source_target_pairs={{0,1},{1,0},{2,3},{3,2},{4,5},{5,4},{6,7},{7,6},{8,9},{9,8},{10,11... | collective-permute-start | bytes 6291464 | tf_op jit(solution)/shard_map/ppermute | solution.py:310
  387.2 140.4 %reduce-scatter.16.cloned.1.call-start = ((), (), s32[]{:S(2)}) async-start(), calls=%async_computation.12 | async-start | bytes 557056
  392.3 2.5 copy-start.18
  392.3 38.1 %copy-start.16 = (bf16[1024,1024]{1,0:T(8,128)(2,1)S(1)}, bf16[1024,1024]{1,0:T(8,128)(2,1)}, u32[]{:S(2)}) copy-start(bf16[1024,1024]{1,0:T(8,128)(2,1)} %param.26) | copy-start | bytes 6291460
  437.1 12.4 %copy-start.12 = (bf16[2048,512]{1,0:T(8,128)(2,1)S(1)}, bf16[2048,512]{1,0:T(8,128)(2,1)}, u32[]{:S(2)}) copy-start(bf16[2048,512]{1,0:T(8,128)(2,1)} %copy-done.10) | copy-start | bytes 6291460
  437.1 134.8 %reduce-scatter.12.cloned.1.call-start = ((), (), s32[]{:S(2)}) async-start(), calls=%async_computation.10 | async-start | bytes 3342336 | tf_op jit(solution)/shard_map/reduce_scatter | solution.py:347
  449.5 7.0 %copy-start.49 = (bf16[1024,2048]{1,0:T(8,128)(2,1)S(1)}, bf16[1024,2048]{1,0:T(8,128)(2,1)}, u32[]{:S(2)}) copy-start(bf16[1024,2048]{1,0:T(8,128)(2,1)} %all-gather.9.cloned.1.call-done.out_ref) | copy-start | bytes 12582916
  469.2 3.3 copy-start.21
  472.5 3.2 copy-start.22
  472.5 3.2 copy-start.29
  472.5 3.2 copy-start.30
  472.5 3.2 copy-start.33
  472.5 4.7 copy-start.23
  472.5 4.7 copy-start.31
  472.5 4.6 copy-start.32
  472.6 4.6 copy-start.34
  474.2 4.4 copy-start.28
  474.2 4.4 copy-start.41
  474.2 4.4 copy-start.42
  474.2 47.4 %copy-start.20 = (bf16[1024,1024]{1,0:T(8,128)(2,1)S(1)}, bf16[1024,1024]{1,0:T(8,128)(2,1)}, u32[]{:S(2)}) copy-start(bf16[1024,1024]{1,0:T(8,128)(2,1)} %param.25) | copy-start | bytes 6291460
  474.2 47.4 %copy-start.44 = (f32[1024,1]{0,1:T(1,128)S(1)}, f32[1024,1]{0,1:T(1,128)}, u32[]{:S(2)}) copy-start(f32[1024,1]{0,1:T(1,128)} %get-tuple-element.97) | copy-start | bytes 12292
  474.2 47.4 %copy-start.45 = (f32[1024,1]{0,1:T(1,128)S(1)}, f32[1024,1]{0,1:T(1,128)}, u32[]{:S(2)}) copy-start(f32[1024,1]{0,1:T(1,128)} %get-tuple-element.98) | copy-start | bytes 12292
  474.3 47.4 %collective-permute-start.2 = (bf16[1024,1024]{1,0:T(8,128)(2,1)}, bf16[1024,1024]{1,0:T(8,128)(2,1)}, u32[]{:S(2)}, u32[]{:S(2)}) collective-permute-start(bf16[1024,1024]{1,0:T(8,128)(2,1)} %dynamic-slice_convert_fusion.1), channel_id=1, source_target_pairs={{0,1},{1,0},{2,3},{3,2},{4,5},{5,4},{6,7},{7,6},{8,9},{9,8},{10,11... | collective-permute-start | bytes 6291464 | tf_op jit(solution)/shard_map/ppermute | solution.py:310
  521.6 11.8 %copy-start.43 = (f32[64,13]{0,1:T(8,128)S(1)}, f32[64,13]{0,1:T(8,128)}, u32[]{:S(2)}) copy-start(f32[64,13]{0,1:T(8,128)} %param.35) | copy-start | bytes 9988
  521.7 11.7 %copy-start.46 = (f32[64,13]{0,1:T(8,128)S(1)}, f32[64,13]{0,1:T(8,128)}, u32[]{:S(2)}) copy-start(f32[64,13]{0,1:T(8,128)} %param.49) | copy-start | bytes 9988
  521.7 11.7 %copy-start.47 = (f32[64,13]{0,1:T(8,128)S(1)}, f32[64,13]{0,1:T(8,128)}, u32[]{:S(2)}) copy-start(f32[64,13]{0,1:T(8,128)} %param.42) | copy-start | bytes 9988
  521.7 50.3 %copy-start.25 = (f32[64,512]{1,0:T(8,128)S(1)}, f32[64,512]{1,0:T(8,128)}, u32[]{:S(2)}) copy-start(f32[64,512]{1,0:T(8,128)} %param.31) | copy-start | bytes 393220
  521.7 50.2 %copy-start.26 = (f32[64,512]{1,0:T(8,128)S(1)}, f32[64,512]{1,0:T(8,128)}, u32[]{:S(2)}) copy-start(f32[64,512]{1,0:T(8,128)} %param.30) | copy-start | bytes 393220
  521.7 50.2 %copy-start.27 = (f32[64,512]{1,0:T(8,128)S(1)}, f32[64,512]{1,0:T(8,128)}, u32[]{:S(2)}) copy-start(f32[64,512]{1,0:T(8,128)} %param.29) | copy-start | bytes 393220
  521.7 50.2 %copy-start.35 = (f32[64,512]{1,0:T(8,128)S(1)}, f32[64,512]{1,0:T(8,128)}, u32[]{:S(2)}) copy-start(f32[64,512]{1,0:T(8,128)} %param.45) | copy-start | bytes 393220
  521.7 50.2 %copy-start.36 = (f32[64,512]{1,0:T(8,128)S(1)}, f32[64,512]{1,0:T(8,128)}, u32[]{:S(2)}) copy-start(f32[64,512]{1,0:T(8,128)} %param.38) | copy-start | bytes 393220
  521.7 50.2 %copy-start.37 = (f32[64,512]{1,0:T(8,128)S(1)}, f32[64,512]{1,0:T(8,128)}, u32[]{:S(2)}) copy-start(f32[64,512]{1,0:T(8,128)} %param.43) | copy-start | bytes 393220
  521.8 50.2 %copy-start.38 = (f32[64,512]{1,0:T(8,128)S(1)}, f32[64,512]{1,0:T(8,128)}, u32[]{:S(2)}) copy-start(f32[64,512]{1,0:T(8,128)} %param.36) | copy-start | bytes 393220
  521.8 50.2 %copy-start.39 = (f32[64,512]{1,0:T(8,128)S(1)}, f32[64,512]{1,0:T(8,128)}, u32[]{:S(2)}) copy-start(f32[64,512]{1,0:T(8,128)} %param.44) | copy-start | bytes 393220
  521.8 50.2 %copy-start.40 = (f32[64,512]{1,0:T(8,128)S(1)}, f32[64,512]{1,0:T(8,128)}, u32[]{:S(2)}) copy-start(f32[64,512]{1,0:T(8,128)} %param.37) | copy-start | bytes 393220
Sparse Core Ops, SparseCore 0:
  10.8 53.5 all-gather.6
  67.1 49.0 all-gather.8
  118.9 49.2 all-gather.4
  171.9 70.8 reduce-scatter.7
  246.9 71.4 reduce-scatter.9
  387.3 56.6 reduce-scatter.13
  448.0 54.7 reduce-scatter.15
  506.6 65.2 reduce-scatter.11
